TPU v7x, 256 devices: a whole 4x4x8 slice. The times are simulated.
256 devices in a mesh: dp: 8 (over z), mp: 16 (over x, y), section: 2 (over core).
Axes of the slice: x: 4, y: 4, z: 8, core: 2. Of those that a mesh axis runs over, the one named last changes fastest.
Arguments:
- encoded: bfloat16 [8192, 6144], P(('dp', 'section'), 'mp'), may hold values from -6 to 6
- visible: int32 [32, 256], P(('dp', 'section')), may hold values from 0 to 1023, as said below
- owner: int32 [1024], replicated, may hold values from 0 to 15, as said below
- embed_weight: bfloat16 [6144, 1024], P('mp'), may hold values from -0.078125 to 0.078125
- mask_token: float32 [1024], replicated, may hold values from -4 to 4
- norm_gain: float32 [1024], replicated, may hold values from 0.5 to 1.5
- query_weight: bfloat16 [1024, 1024], replicated, may hold values from -0.1875 to 0.1875
- key_weight: bfloat16 [1024, 1024], replicated, may hold values from -0.1875 to 0.1875
- value_weight: bfloat16 [1024, 1024], replicated, may hold values from -0.1875 to 0.1875
- out_weight: bfloat16 [1024, 1024], replicated, may hold values from -0.1875 to 0.1875
- pixel_weight: bfloat16 [1024, 768], replicated, may hold values from -0.1875 to 0.1875
- targets: bfloat16 [32, 1024, 768], P(('dp', 'section'), 'mp'), may hold values from -6 to 6
Outputs:
- predicted: bfloat16 [32, 1024, 768], P(('dp', 'section'), 'mp')
- encoded_grad: bfloat16 [8192, 6144], P(('dp', 'section'), 'mp')
- embed_grad: float32 [6144, 1024], P('mp')
Inputs may be any that keep to these rules, and one draw needn't show every extreme that they name: Every owner holds exactly 64 patches. `visible`: each image names 256 different patches; in each image at most 32 of them belong to one owner, exactly 32 to some owner and none to some other owner.
All inputs are finite; a program needn't handle non-finite values.
Results may differ from a plain program's by a relative error of at most 0.04.
Values may be sent and summed in bfloat16 or wider, within the bound.
A program may use at most 192 MiB of HBM per device.

v0:
```python
import jax
import jax.numpy as jnp
from jax import lax
from jax.sharding import PartitionSpec as P

HEADS = 16
GRID = 32


def sincos_table(patch_index, dec_width):
    quarter = dec_width // 4
    freqs = 10000.0 ** (-jnp.arange(quarter, dtype=jnp.float32) / quarter)
    row_pos = (patch_index // GRID).astype(jnp.float32)[:, None] * freqs[None, :]
    col_pos = (patch_index % GRID).astype(jnp.float32)[:, None] * freqs[None, :]
    return jnp.concatenate(
        [jnp.sin(row_pos), jnp.cos(row_pos), jnp.sin(col_pos), jnp.cos(col_pos)], axis=1
    )


def prior_count(labels, span):
    onehot = (labels[..., None] == jnp.arange(span, dtype=jnp.int32)).astype(jnp.int32)
    return jnp.sum((jnp.cumsum(onehot, axis=-2) - onehot) * onehot, axis=-1)


def project(left, weight):
    return jnp.einsum("bse,ef->bsf", left, weight, preferred_element_type=jnp.float32)


def project_back(left, weight):
    return jnp.einsum("bsf,ef->bse", left, weight, preferred_element_type=jnp.float32)


def body(
    encoded,
    visible,
    owner,
    embed_weight,
    mask_token,
    norm_gain,
    query_weight,
    key_weight,
    value_weight,
    out_weight,
    pixel_weight,
    targets,
):
    owners = lax.axis_size("mp")
    my_owner = lax.axis_index("mp")
    images, shown = visible.shape
    patches = owner.shape[0]
    per_owner = patches // owners
    capacity = 2 * shown // owners
    dec_width = query_weight.shape[0]
    head_dim = dec_width // HEADS
    score_scale = head_dim ** (-0.5)
    row_count = images * shown
    patch_rank = prior_count(owner, owners)
    row_owner = jnp.take(owner, visible)
    row_rank = jnp.take(patch_rank, visible)
    row_slot = prior_count(row_owner, owners)
    image_of_row = jnp.broadcast_to(jnp.arange(images, dtype=jnp.int32)[:, None], (images, shown))
    slot_ids = ((row_owner * images + image_of_row) * capacity + row_slot).reshape(-1)
    total_slots = owners * images * capacity
    source = (
        jnp.zeros((total_slots,), jnp.int32)
        .at[slot_ids]
        .set(jnp.arange(row_count, dtype=jnp.int32))
    )
    filled = jnp.zeros((total_slots,), jnp.int32).at[slot_ids].set(1)
    projected = jnp.dot(encoded, embed_weight, preferred_element_type=jnp.float32)
    slots_in = (
        lax.psum_scatter(
            jnp.where(filled[:, None] > 0, jnp.take(projected, source, axis=0), 0.0).astype(
                jnp.bfloat16
            ),
            "mp",
            scatter_dimension=0,
            tiled=True,
        )
        .astype(jnp.float32)
        .reshape(images, capacity, dec_width)
    )
    is_mine = row_owner == my_owner
    spot_ids = jnp.arange(per_owner, dtype=jnp.int32)
    at_spot = is_mine[:, :, None] & (row_rank[:, :, None] == spot_ids[None, None, :])
    seen = jnp.any(at_spot, axis=1)
    slot_at = jnp.sum(jnp.where(at_spot, row_slot[:, :, None], 0), axis=1)
    gathered_in = jnp.take_along_axis(slots_in, slot_at[:, :, None], axis=1)
    owned_hit = (owner[None, :] == my_owner) & (patch_rank[None, :] == spot_ids[:, None])
    local_patch = jnp.sum(
        jnp.where(owned_hit, jnp.arange(patches, dtype=jnp.int32)[None, :], 0), axis=1
    )
    inputs = (
        jnp.where(seen[:, :, None], gathered_in, mask_token[None, None, :])
        + sincos_table(local_patch, dec_width)[None]
    )
    average = jnp.mean(inputs, axis=-1, keepdims=True)
    centered = inputs - average
    inv_std = lax.rsqrt(jnp.mean(centered * centered, axis=-1, keepdims=True) + 1e-06)
    standard = centered * inv_std
    normed = (standard * norm_gain).astype(jnp.bfloat16)
    queries = project(normed, query_weight).astype(jnp.bfloat16)
    keys_own = project(normed, key_weight).astype(jnp.bfloat16)
    values_own = project(normed, value_weight).astype(jnp.bfloat16)
    all_keys, all_values = (
        lax.all_gather(keys_own[None], "mp", axis=0, tiled=True),
        lax.all_gather(values_own[None], "mp", axis=0, tiled=True),
    )
    query_heads = queries.reshape(images, per_owner, HEADS, head_dim)
    key_heads = all_keys.reshape(owners, images, per_owner, HEADS, head_dim)
    value_heads = all_values.reshape(owners, images, per_owner, HEADS, head_dim)
    scores = (
        jnp.einsum("bqhd,jbkhd->bhqjk", query_heads, key_heads, preferred_element_type=jnp.float32)
        * score_scale
    )
    row_max = jnp.max(scores, axis=(3, 4), keepdims=True)
    exp_scores = jnp.exp(scores - row_max)
    totals = jnp.sum(exp_scores, axis=(3, 4), keepdims=True)
    attn_probs = exp_scores / totals
    probs_low = attn_probs.astype(jnp.bfloat16)
    attended = jnp.einsum(
        "bhqjk,jbkhd->bqhd", probs_low, value_heads, preferred_element_type=jnp.float32
    ).astype(jnp.bfloat16)
    attended_flat = attended.reshape(images, per_owner, dec_width)
    updated = inputs + project(attended_flat, out_weight)
    pixels = project(updated.astype(jnp.bfloat16), pixel_weight)
    predicted = pixels.astype(jnp.bfloat16)
    residual_px = jnp.where(seen[:, :, None], 0.0, pixels - targets.astype(jnp.float32)).astype(
        jnp.bfloat16
    )
    grad_updated = project_back(residual_px, pixel_weight)
    grad_attended = project_back(grad_updated.astype(jnp.bfloat16), out_weight).astype(jnp.bfloat16)
    grad_heads = grad_attended.reshape(images, per_owner, HEADS, head_dim)
    delta_sum = jnp.sum(grad_heads.astype(jnp.float32) * attended.astype(jnp.float32), axis=-1)
    grad_probs = jnp.einsum(
        "bqhd,jbkhd->bhqjk", grad_heads, value_heads, preferred_element_type=jnp.float32
    )
    delta_wide = jnp.transpose(delta_sum, (0, 2, 1))[:, :, :, None, None]
    grad_scores = (attn_probs * (grad_probs - delta_wide) * score_scale).astype(jnp.bfloat16)
    grad_queries = jnp.einsum(
        "bhqjk,jbkhd->bqhd", grad_scores, key_heads, preferred_element_type=jnp.float32
    )
    grad_queries = grad_queries.astype(jnp.bfloat16).reshape(images, per_owner, dec_width)
    block_rows = images * per_owner
    key_part = jnp.einsum(
        "bhqjk,bqhd->jbkhd", grad_scores, query_heads, preferred_element_type=jnp.float32
    ).reshape(block_rows * lax.axis_size("mp"), dec_width)
    value_part = jnp.einsum(
        "bhqjk,bqhd->jbkhd", probs_low, grad_heads, preferred_element_type=jnp.float32
    ).reshape(block_rows * lax.axis_size("mp"), dec_width)
    summed = (
        lax.psum_scatter(
            jnp.concatenate([key_part, value_part], axis=1).astype(jnp.bfloat16),
            "mp",
            scatter_dimension=0,
            tiled=True,
        )
        .astype(jnp.float32)
        .reshape(images, per_owner, 2 * dec_width)
    )
    grad_keys = summed[:, :, :dec_width].astype(jnp.bfloat16)
    grad_values = summed[:, :, dec_width:].astype(jnp.bfloat16)
    grad_normed = (
        project_back(grad_queries, query_weight)
        + project_back(grad_keys, key_weight)
        + project_back(grad_values, value_weight)
    )
    scaled = grad_normed * norm_gain
    grad_inputs = grad_updated + inv_std * (
        scaled
        - jnp.mean(scaled, axis=-1, keepdims=True)
        - standard * jnp.mean(scaled * standard, axis=-1, keepdims=True)
    )
    slot_hot = is_mine[:, :, None] & (
        row_slot[:, :, None] == jnp.arange(capacity, dtype=jnp.int32)[None, None, :]
    )
    slot_spot = jnp.sum(jnp.where(slot_hot, row_rank[:, :, None], 0), axis=1)
    slot_live = jnp.any(slot_hot, axis=1)
    slots_out = jnp.where(
        slot_live[:, :, None], jnp.take_along_axis(grad_inputs, slot_spot[:, :, None], axis=1), 0.0
    ).astype(jnp.bfloat16)
    flat_owner = row_owner.reshape(-1)
    flat_slot = row_slot.reshape(-1)
    flat_image = image_of_row.reshape(-1)
    shard_piece = lax.all_gather(slots_out[None], "mp", axis=0, tiled=True)
    piece_count = shard_piece.shape[0]
    inside = (flat_owner >= 0) & (flat_owner < piece_count)
    values_back = shard_piece[jnp.clip(flat_owner, 0, piece_count - 1), flat_image, flat_slot]
    returned = jnp.where(
        inside[:, None], values_back, jnp.zeros((row_count, dec_width), jnp.bfloat16)
    )
    encoded_grad = jnp.einsum(
        "re,de->rd", returned, embed_weight, preferred_element_type=jnp.float32
    ).astype(jnp.bfloat16)
    embed_local = jnp.einsum("rd,re->de", encoded, returned, preferred_element_type=jnp.float32)
    groups = lax.axis_size(("dp", "section"))
    embed_grad = lax.psum(embed_local.astype(jnp.bfloat16), ("dp", "section")).astype(
        jnp.float32
    ) * (row_count * groups) ** (-0.5)
    return (predicted, encoded_grad, embed_grad)


def solution(mesh):
    placed = (
        P(("dp", "section"), "mp"),
        P(("dp", "section"), None),
        P(),
        P("mp", None),
        P(),
        P(),
        P(),
        P(),
        P(),
        P(),
        P(),
        P(("dp", "section"), "mp", None),
    )
    return jax.shard_map(
        body,
        mesh=mesh,
        in_specs=placed,
        out_specs=(P(("dp", "section"), "mp", None), P(("dp", "section"), "mp"), P("mp", None)),
        check_vma=False,
    )
```

profile of v0, /device:TPU:1, one launch (start us, length us, event | category | flops | bytes accessed | tf_op | source)
XLA Modules:
  0.0 648.8 jit_solution(4799725753279273139)
XLA Ops:
  8.1 3.4 gather_fusion.4
  21.8 5.4 gather_fusion
  27.2 3.3 select_convert_fusion
  30.6 4.5 reduce-window.14
  39.0 73.2 %reduce-scatter.3.cloned.1.call-done = bf16[64,1024]{1,0:T(8,128)(2,1)} async-done(((bf16[1024,1024]{1,0:T(8,128)(2,1)}), bf16[64,1024]{1,0:T(8,128)(2,1)}) %reduce-scatter.3.cloned.1.call-update) | async-done | bytes 131088 | tf_op jit(solution)/shard_map/reduce_scatter | solution.py:72
  115.3 2.7 fusion.60
  118.1 2.7 fusion.54
  125.7 49.9 %all-gather.10.cloned.1.call-done = bf16[32,64,1024]{2,1,0:T(8,128)(2,1)} async-done(((bf16[2,64,1024]{2,1,0:T(8,128)(2,1)}), bf16[32,64,1024]{2,1,0:T(8,128)(2,1)}) %all-gather.10.cloned.1.call-update) | async-done | bytes 4194320 | tf_op jit(solution)/shard_map/all_gather | solution.py:106
  175.7 11.6 %reshape.346 = bf16[16,2,64,16,64]{4,3,2,1,0:T(8,128)(2,1)} reshape(bf16[32,64,1024]{2,1,0:T(8,128)(2,1)} %all-gather.10.cloned.1.call-done) | data formatting | bytes 8388608 | tf_op jit(solution)/shard_map/reshape | solution.py:110
  187.3 12.5 %copy.104 = bf16[16,2,64,16,64]{2,4,0,3,1:T(8,128)(2,1)} copy(bf16[16,2,64,16,64]{4,3,2,1,0:T(8,128)(2,1)} %reshape.346) | data formatting | bytes 8388608 | tf_op jit(solution)/shard_map/reshape | solution.py:110
  199.8 12.7 %multiply_reduce_fusion = (f32[2,16,64]{2,1,0:T(8,128)S(1)}, f32[2,16,64,16,64]{2,4,3,1,0:T(8,128)}) fusion(bf16[2,64,16,64,1]{1,3,4,2,0:T(8,128)(2,1)S(1)} %copy.122, bf16[16,2,64,16,64]{2,4,0,3,1:T(8,128)(2,1)} %copy.104), kind=kOutput, calls=%fused_computation.10 | convolution fusion | flops 272627712 | bytes 12853248 | tf_op jit(solution)/shard_map/bqhd,jbkhd->bhqjk/dot_general | solution.py:113
  212.4 9.5 %fusion.1 = f32[2,16,64]{2,1,0:T(8,128)S(1)} fusion(f32[2,16,64,16,64]{2,4,3,1,0:T(8,128)} %get-tuple-element.36, f32[2,16,64]{2,1,0:T(8,128)S(1)} %get-tuple-element.35), kind=kLoop, calls=%fused_computation.12 | loop fusion | flops 6289408 | bytes 8404992 | tf_op jit(solution)/shard_map/reduce_sum | solution.py:118
  221.9 13.4 %all-gather.8.cloned.1.call-done = bf16[32,64,1024]{2,1,0:T(8,128)(2,1)} async-done(((bf16[2,64,1024]{2,1,0:T(8,128)(2,1)}), bf16[32,64,1024]{2,1,0:T(8,128)(2,1)}) %all-gather.8.cloned.1.call-update) | async-done | bytes 4194320 | tf_op jit(solution)/shard_map/all_gather | solution.py:107
  235.3 11.6 %reshape.344 = bf16[16,2,64,16,64]{4,3,2,1,0:T(8,128)(2,1)} reshape(bf16[32,64,1024]{2,1,0:T(8,128)(2,1)} %all-gather.8.cloned.1.call-done) | data formatting | bytes 8388608 | tf_op jit(solution)/shard_map/reshape | solution.py:111
  246.9 12.5 %fusion.35 = bf16[2,16,64,64]{3,2,1,0:T(8,128)(2,1)} fusion(bf16[16,2,64,16,64]{4,3,2,1,0:T(8,128)(2,1)} %reshape.344, f32[2,16,64,16,64]{2,4,3,1,0:T(8,128)} %get-tuple-element.36, f32[2,16,64]{2,1,0:T(8,128)S(1)} %fusion.1, f32[2,16,64]{2,1,0:T(8,128)S(1)} %get-tuple-element.35), kind=kOutput, calls=%fused_computation.47 | convolution fusion | flops 276955136 | bytes 12861440 | tf_op jit(solution)/shard_map/bhqjk,jbkhd->bqhd/dot_general | solution.py:121
  259.4 3.1 fusion.118
  267.9 13.6 %convert_bitcast_fusion = bf16[16,2,64,16,64]{2,4,0,3,1:T(8,128)(2,1)} fusion(bf16[2,64,16,64,1]{1,3,4,2,0:T(8,128)(2,1)S(1)} %bitcast.187, f32[2,16,64,16,64]{2,4,3,1,0:T(8,128)} %get-tuple-element.36, f32[2,16,64]{2,1,0:T(8,128)} %copy-done.16, f32[2,16,64]{2,1,0:T(8,128)} %copy-done.7), kind=kOutput, calls=%fused_computation.14 | convolution fusion | flops 278921216 | bytes 12861440 | tf_op jit(solution)/shard_map/bhqjk,bqhd->jbkhd/dot_general | solution.py:148
  281.6 13.6 %multiply_convert_fusion = bf16[2,16,64,16,64]{2,4,3,1,0:T(8,128)(2,1)} fusion(f32[2,16,64]{2,1,0:T(8,128)S(1)} %bitcast.198, bf16[2,64,16,64,1]{1,3,4,2,0:T(8,128)(2,1)S(1)} %bitcast.188, bf16[16,2,64,16,64]{4,3,2,1,0:T(8,128)(2,1)} %reshape.344, f32[2,16,64]{2,1,0:T(8,128)S(1)} %copy-done.17, f32[2,16,64]{2,1,0:T(8,128)S(1)} %copy-done.8, ...), kind=kOutput, calls=%fused_computation.8 | convolution fusion | flops 283115520 | bytes 17063936 | tf_op jit(solution)/shard_map/bqhd,jbkhd->bhqjk/dot_general | solution.py:135
  295.2 14.7 %convert_bitcast_fusion.1 = bf16[16,2,64,16,64]{2,4,0,3,1:T(8,128)(2,1)} fusion(bf16[2,64,16,64,1]{1,3,4,2,0:T(8,128)(2,1)S(1)} %copy.122, bf16[2,16,64,16,64]{2,4,3,1,0:T(8,128)(2,1)} %multiply_convert_fusion), kind=kOutput, calls=%fused_computation.15 | convolution fusion | flops 270532608 | bytes 8650752 | tf_op jit(solution)/shard_map/bhqjk,bqhd->jbkhd/dot_general | solution.py:145
  309.9 13.1 %copy.109 = bf16[16,2,64,16,64]{4,3,2,1,0:T(8,128)(2,1)} copy(bf16[16,2,64,16,64]{2,4,0,3,1:T(8,128)(2,1)} %convert_bitcast_fusion.1) | data formatting | bytes 8388608 | tf_op jit(solution)/shard_map/bhqjk,bqhd->jbkhd/transpose | solution.py:145
  323.0 11.9 %reshape.350 = bf16[2048,1024]{1,0:T(8,128)(2,1)} reshape(bf16[16,2,64,16,64]{4,3,2,1,0:T(8,128)(2,1)} %copy.109) | data formatting | bytes 8388608 | tf_op jit(solution)/shard_map/reshape | solution.py:147
  334.9 13.1 %copy.111 = bf16[16,2,64,16,64]{4,3,2,1,0:T(8,128)(2,1)} copy(bf16[16,2,64,16,64]{2,4,0,3,1:T(8,128)(2,1)} %convert_bitcast_fusion) | data formatting | bytes 8388608 | tf_op jit(solution)/shard_map/bhqjk,bqhd->jbkhd/transpose | solution.py:148
  348.0 11.9 %reshape.351 = bf16[2048,1024]{1,0:T(8,128)(2,1)} reshape(bf16[16,2,64,16,64]{4,3,2,1,0:T(8,128)(2,1)} %copy.111) | data formatting | bytes 8388608 | tf_op jit(solution)/shard_map/reshape | solution.py:150
  359.9 8.1 %pad_maximum_fusion = bf16[2048,2048]{1,0:T(8,128)(2,1)} fusion(bf16[2048,1024]{1,0:T(8,128)(2,1)} %reshape.351, bf16[2048,1024]{1,0:T(8,128)(2,1)} %reshape.350), kind=kLoop, calls=%fused_computation.13 | loop fusion | flops 16777216 | bytes 16777216 | tf_op jit(solution)/shard_map/concatenate | solution.py:153
  369.7 8.6 %fusion.41 = bf16[2,16,64,64]{3,2,1,0:T(8,128)(2,1)} fusion(bf16[16,2,64,16,64]{2,4,0,3,1:T(8,128)(2,1)} %copy.104, bf16[2,16,64,16,64]{2,4,3,1,0:T(8,128)(2,1)} %multiply_convert_fusion), kind=kOutput, calls=%fused_computation.49 | convolution fusion | flops 268566528 | bytes 8650752 | tf_op jit(solution)/shard_map/bhqjk,jbkhd->bqhd/dot_general | solution.py:140
  378.3 78.2 %reduce-scatter.5.cloned.1.call-done = bf16[128,2048]{1,0:T(8,128)(2,1)} async-done(((bf16[2048,2048]{1,0:T(8,128)(2,1)}), bf16[128,2048]{1,0:T(8,128)(2,1)}) %reduce-scatter.5.cloned.1.call-update) | async-done | bytes 524304 | tf_op jit(solution)/shard_map/reduce_scatter | solution.py:152
  461.0 2.6 fusion.116
  467.9 48.7 %all-gather.6.cloned.1.call-done = bf16[16,2,32,1024]{3,2,1,0:T(8,128)(2,1)} async-done(((bf16[1,2,32,1024]{3,2,1,0:T(8,128)(2,1)}), bf16[16,2,32,1024]{3,2,1,0:T(8,128)(2,1)}) %all-gather.6.cloned.1.call-update) | async-done | bytes 2097168 | tf_op jit(solution)/shard_map/all_gather | solution.py:185
  516.5 6.9 %gather_fusion.1 = bf16[512,1024]{1,0:T(8,128)(2,1)S(1)} fusion(bf16[16,2,32,1024]{3,2,1,0:T(8,128)(2,1)} %all-gather.6.cloned.1.call-done, s32[512]{0:T(512)S(1)} %bitcast.185), kind=kCustom, calls=%fused_computation.3 | custom fusion | bytes 2103296 | tf_op jit(solution)/shard_map/gather | solution.py:188
  525.2 2.6 convolution_convert_fusion.1
  527.9 108.5 %all-reduce.2.cloned.1.call-done = bf16[384,1024]{0,1:T(8,128)(2,1)} async-done(((bf16[384,1024]{0,1:T(8,128)(2,1)}), bf16[384,1024]{0,1:T(8,128)(2,1)}) %all-reduce.2.cloned.1.call-update) | async-done | bytes 786448 | tf_op jit(solution)/shard_map/psum | solution.py:197
  638.8 3.0 copy.112
  (129 shorter events, 43.0 us)
Async XLA Ops:
  7.2 252.3 %copy-start = (bf16[1024,1024]{1,0:T(8,128)(2,1)S(1)}, bf16[1024,1024]{1,0:T(8,128)(2,1)}, u32[]{:S(2)}) copy-start(bf16[1024,1024]{1,0:T(8,128)(2,1)} %param.23) | copy-start | bytes 6291460
  7.2 105.0 %reduce-scatter.3.cloned.1.call-start = ((), (), s32[]{:S(2)}) async-start(), calls=%async_computation.2 | async-start | bytes 2228224 | tf_op jit(solution)/shard_map/reduce_scatter | solution.py:72
  21.8 8.7 %copy-start.2 = (s32[1024]{0:T(1024)S(1)}, s32[1024]{0:T(1024)}, u32[]{:S(2)}) copy-start(s32[1024]{0:T(1024)} %param.16) | copy-start | bytes 12292
  27.2 10.7 %copy-start.11 = (s32[2,256]{1,0:T(2,128)S(1)}, s32[2,256]{1,0:T(2,128)}, u32[]{:S(2)}) copy-start(s32[2,256]{1,0:T(2,128)} %param.15) | copy-start | bytes 6148
  27.2 87.5 %copy-start.18 = (f32[1024]{0:T(1024)S(1)}, f32[1024]{0:T(1024)}, u32[]{:S(2)}) copy-start(f32[1024]{0:T(1024)} %param.18) | copy-start | bytes 12292
  27.2 87.9 %copy-start.12 = (f32[1024]{0:T(1024)S(1)}, f32[1024]{0:T(1024)}, u32[]{:S(2)}) copy-start(f32[1024]{0:T(1024)} %param.19) | copy-start | bytes 12292
  30.5 145.2 %all-gather.10.cloned.1.call-start = ((), (), s32[]{:S(2)}) async-start(), calls=%async_computation.7 | async-start | bytes 4456448 | tf_op jit(solution)/shard_map/all_gather | solution.py:106
  114.9 6.0 copy-start.9
  115.1 72.2 %copy-start.14 = (f32[2,64]{1,0:T(2,128)}, f32[2,64]{1,0:T(2,128)S(1)}, u32[]{:S(2)}) copy-start(f32[2,64]{1,0:T(2,128)S(1)} %add_rsqrt_fusion) | copy-start | bytes 1540
  118.0 117.3 %all-gather.8.cloned.1.call-start = ((), (), s32[]{:S(2)}) async-start(), calls=%async_computation.6 | async-start | bytes 4456448 | tf_op jit(solution)/shard_map/all_gather | solution.py:107
  120.9 335.6 %reduce-scatter.5.cloned.1.call-start = ((), (), s32[]{:S(2)}) async-start(), calls=%async_computation.3 | async-start | bytes 8912896 | tf_op jit(solution)/shard_map/reduce_scatter | solution.py:152
  212.4 34.5 %copy-start.7 = (f32[2,16,64]{2,1,0:T(8,128)}, f32[2,16,64]{2,1,0:T(8,128)S(1)}, u32[]{:S(2)}) copy-start(f32[2,16,64]{2,1,0:T(8,128)S(1)} %get-tuple-element.35) | copy-start | bytes 24580
  221.9 37.5 %copy-start.16 = (f32[2,16,64]{2,1,0:T(8,128)}, f32[2,16,64]{2,1,0:T(8,128)S(1)}, u32[]{:S(2)}) copy-start(f32[2,16,64]{2,1,0:T(8,128)S(1)} %fusion.1) | copy-start | bytes 24580
  264.7 0.8 copy-start.4
  267.9 13.7 %copy-start.8 = (f32[2,16,64]{2,1,0:T(8,128)S(1)}, f32[2,16,64]{2,1,0:T(8,128)}, u32[]{:S(2)}) copy-start(f32[2,16,64]{2,1,0:T(8,128)} %copy-done.7) | copy-start | bytes 24580
  267.9 13.7 %copy-start.17 = (f32[2,16,64]{2,1,0:T(8,128)S(1)}, f32[2,16,64]{2,1,0:T(8,128)}, u32[]{:S(2)}) copy-start(f32[2,16,64]{2,1,0:T(8,128)} %copy-done.16) | copy-start | bytes 24580
  368.0 148.5 %all-gather.6.cloned.1.call-start = ((), (), s32[]{:S(2)}) async-start(), calls=%async_computation.4 | async-start | bytes 2228224 | tf_op jit(solution)/shard_map/all_gather | solution.py:185
  369.7 89.3 %copy-start.3 = (bf16[1024,1024]{1,0:T(8,128)(2,1)S(1)}, bf16[1024,1024]{1,0:T(8,128)(2,1)}, u32[]{:S(2)}) copy-start(bf16[1024,1024]{1,0:T(8,128)(2,1)} %param.20) | copy-start | bytes 6291460
  369.7 91.2 %copy-start.10 = (f32[2,64]{1,0:T(2,128)S(1)}, f32[2,64]{1,0:T(2,128)}, u32[]{:S(2)}) copy-start(f32[2,64]{1,0:T(2,128)} %copy-done.9) | copy-start | bytes 1540
  369.7 91.2 %copy-start.13 = (f32[1024]{0:T(1024)S(1)}, f32[1024]{0:T(1024)}, u32[]{:S(2)}) copy-start(f32[1024]{0:T(1024)} %param.19) | copy-start | bytes 12292
  378.3 85.3 %copy-start.5 = (f32[2,64,1024]{2,1,0:T(8,128)S(1)}, f32[2,64,1024]{2,1,0:T(8,128)}, u32[]{:S(2)}) copy-start(f32[2,64,1024]{2,1,0:T(8,128)} %copy-done.4) | copy-start | bytes 1572868
  456.5 7.1 %copy-start.15 = (f32[2,64]{1,0:T(2,128)S(1)}, f32[2,64]{1,0:T(2,128)}, u32[]{:S(2)}) copy-start(f32[2,64]{1,0:T(2,128)} %copy-done.14) | copy-start | bytes 1540
  461.0 62.5 %copy-start.6 = (bf16[512,384]{1,0:T(8,128)(2,1)S(1)}, bf16[512,384]{1,0:T(8,128)(2,1)}, u32[]{:S(2)}) copy-start(bf16[512,384]{1,0:T(8,128)(2,1)} %param.14) | copy-start | bytes 1179652
  466.4 169.9 %all-reduce.2.cloned.1.call-start = ((), (), s32[]{:S(2)}) async-start(), calls=%async_computation.5 | async-start | bytes 1572864 | tf_op jit(solution)/shard_map/psum | solution.py:197
  516.5 125.2 %copy-start.1 = (bf16[1024,1024]{1,0:T(8,128)(2,1)S(1)}, bf16[1024,1024]{1,0:T(8,128)(2,1)}, u32[]{:S(2)}) copy-start(bf16[1024,1024]{1,0:T(8,128)(2,1)} %param.23) | copy-start | bytes 6291460
Sparse Core Ops, SparseCore 0:
  30.6 81.5 reduce-scatter.2
  118.1 57.5 all-gather.9
  179.0 56.2 all-gather.7
  368.2 88.2 reduce-scatter.4
  466.5 49.9 all-gather.5
  525.3 110.9 all-reduce.1
where the time goes:
time: 658 us; the launch traced here: 649 us
  waiting for transfers between devices  372 us (57%)
  local copies, waits for them, and re-layouts  120 us (18%)
  matrix products  103 us (16%)
  other arithmetic  38.9 us (6%)
  between operations  14.7 us (2%)
    psum x1, waiting for transfers between devices, body(): lax.psum(embed_local.astype(jnp.bfloat16), ('dp', 'section'))  108 us
    reduce_scatter x1, waiting for transfers between devices, body(): lax.psum_scatter(jnp.concatenate([key_part, value_part], axis=1).astype(j...  78.2 us
    reduce_scatter x1, waiting for transfers between devices, body(): lax.psum_scatter(jnp.where(filled[:, None] > 0, jnp.take(projected, sourc...  73.2 us
    all_gather x1, waiting for transfers between devices, body(): lax.all_gather(keys_own[None], 'mp', axis=0, tiled=True)  49.9 us
    all_gather x1, waiting for transfers between devices, body(): shard_piece = lax.all_gather(slots_out[None], 'mp', axis=0, tiled=True)  48.7 us
    reshape x2, local copies, waits for them, and re-layouts, body(): key_heads = all_keys.reshape(owners, images, per_owner, HEADS, head_dim)  24.1 us
    dot_general x1, matrix products, body(): jnp.einsum('bhqjk,bqhd->jbkhd', grad_scores, query_heads, preferred_eleme...  14.7 us
    dot_general x1, matrix products, body(): jnp.einsum('bhqjk,bqhd->jbkhd', probs_low, grad_heads, preferred_element_...  13.6 us
  transfers between devices with their start and end apart: 6, of which 6 were waited for; matrix products, arithmetic and copies ran while one was open for 12% of the time, Pallas kernels for 0%

commit v1 on v0

v1 whole, which is shorter than its diff:
```python
import functools

import jax
import jax.numpy as jnp
from jax import lax
from jax.experimental import pallas as pl
from jax.experimental.pallas import tpu as pltpu
from jax.sharding import PartitionSpec as P

MESH = pl.DeviceIdType.MESH
F32 = jnp.float32
BF16 = jnp.bfloat16
GRID = 32
N = 16
NZ = 8
HD = 64


def nn(a, b):
    return lax.dot_general(a, b, (((1,), (0,)), ((), ())), preferred_element_type=F32)


def nt(a, b):
    return lax.dot_general(a, b, (((1,), (1,)), ((), ())), preferred_element_type=F32)


def tn(a, b):
    return lax.dot_general(a, b, (((0,), (0,)), ((), ())), preferred_element_type=F32)


def fiota(shape, dim):
    return lax.broadcasted_iota(jnp.int32, shape, dim).astype(F32)


def hot(cond):
    return jnp.where(cond, 1.0, 0.0).astype(BF16)


def norm(x):
    c = x - jnp.mean(x, axis=-1, keepdims=True)
    inv = lax.rsqrt(jnp.mean(c * c, axis=-1, keepdims=True) + 1e-06)
    return c * inv, inv


def rows(i, size):
    return pl.ds(pl.multiple_of(i * size, size), size)


def kernel(
    enc_h, we_h, own_r, vis_r, mask_r, gain_r, wq_h, wk_h, wv_h, wo_h, wp_h, tgt_h, trig_r,
    pred_o, encg_o, emb_o,
    enc, we, wq, wk, wv, wo, wp, tgt,
    part, rsbuf, emb, encT,
    placec, vprow, vpcol, viscol, ptab, pos, xvis, wh, tab, qkvv,
    qf, kf, v2, lse, attp, attb, attf, gsend, gall, dpack, dbuf, df, ret,
    loc, zin, zbuf, zown, zgat, half_in,
    lsem, ssem, rs_s, ag_s, at_s, g_s, d_s, ag2_s, zsend, z1_s, z2_s, csend, crecv,
):
    m = lax.axis_index("mp")
    z = lax.axis_index("dp")
    c = lax.axis_index("section")

    pairs = [(enc_h, enc), (we_h, we), (wq_h, wq), (wk_h, wk), (wv_h, wv), (wo_h, wo), (wp_h, wp), (tgt_h, tgt)]
    loads = [pltpu.make_async_copy(s, d, lsem.at[i]) for i, (s, d) in enumerate(pairs)]
    for load in loads:
        load.start()

    barrier = pltpu.get_barrier_semaphore()

    def greet_mp(j, _):
        pl.semaphore_signal(barrier, inc=1, device_id={"mp": lax.rem(m + j, N)}, device_id_type=MESH)
        return 0

    def greet_z(j, _):
        pl.semaphore_signal(barrier, inc=1, device_id={"dp": lax.rem(z + j, NZ)}, device_id_type=MESH)
        return 0

    lax.fori_loop(1, N, greet_mp, 0)
    lax.fori_loop(1, NZ, greet_z, 0)
    pl.semaphore_signal(barrier, inc=1, device_id={"section": 1 - c}, device_id_type=MESH)

    def copy_to(k, src, dst, recv):
        return pltpu.make_async_remote_copy(
            src_ref=src, dst_ref=dst, send_sem=ssem.at[k], recv_sem=recv,
            device_id={"mp": k}, device_id_type=MESH,
        )

    def wait_sends(src):
        def one(j, _):
            k = lax.rem(m + j, N)
            copy_to(k, src, src, ssem.at[k]).wait_send()
            return 0

        lax.fori_loop(1, N, one, 0)

    def wait_from(k, dst, sems):
        copy_to(k, dst, dst, sems.at[k]).wait_recv()

    loads[0].wait()
    loads[1].wait()

    def partial_block(g):
        part[rows(g, 128), :] = nn(enc[rows(g, 128), :], we[...]).astype(BF16)

    def send_part(k):
        copy_to(k, part.at[rows(k, 32)], rsbuf.at[m], rs_s.at[m]).start()

    my_group = m // 4
    partial_block(lax.rem(my_group + 1, 4))
    pl.semaphore_wait(barrier, N - 1 + NZ - 1 + 1)

    def send_group(jj, _):
        g = lax.rem(my_group + jj, 4)

        @pl.when(jj > 1)
        def _():
            partial_block(g)

        for i in range(4):
            send_part(4 * g + i)
        return 0

    lax.fori_loop(1, 4, send_group, 0)
    partial_block(my_group)
    for i in range(1, 4):
        send_part(4 * my_group + lax.rem(m + i, 4))

    key_row = own_r[...].astype(F32) * 1024.0 + fiota((1, 1024), 1)
    lane = fiota((256, 1024), 1)

    def places(i, place_row):
        s = fiota((256, 1024), 0) + (i * 256).astype(F32)
        key_col = jnp.sum(jnp.where(lane == s, key_row, 0.0), axis=1, keepdims=True)
        less = jnp.where(key_row < key_col, 1.0, 0.0)
        placec[rows(i, 256), :] = jnp.sum(less, axis=1, keepdims=True)
        more = jnp.where(key_col < key_row, 1.0, 0.0)
        return place_row + jnp.sum(more, axis=0, keepdims=True)

    place_row = lax.fori_loop(0, 4, places, jnp.zeros((1, 1024), F32))

    for b in range(2):
        vrow = vis_r[b : b + 1, :].astype(F32)
        vcol = jnp.sum(jnp.where(fiota((256, 256), 0) == fiota((256, 256), 1), vrow, 0.0), axis=1, keepdims=True)
        viscol[b * 256 : (b + 1) * 256, :] = vcol
        vpcol[b * 256 : (b + 1) * 256, :] = jnp.sum(
            jnp.where(lane == vcol, place_row, 0.0), axis=1, keepdims=True
        )
        vprow[b : b + 1, :] = jnp.sum(
            jnp.where(fiota((1024, 256), 0) == vrow, placec[...], 0.0), axis=0, keepdims=True
        )

    trig = trig_r[...]
    hi = trig.astype(BF16)
    rest = trig - hi.astype(F32)
    mid = rest.astype(BF16)
    low = (rest - mid.astype(F32)).astype(BF16)
    ptab[...] = jnp.zeros_like(ptab)
    for i, term in enumerate((hi, mid, low)):
        ptab[32 * i : 32 * i + 32, 0:512] = term
        ptab[96 + 32 * i : 128 + 32 * i, 512:1024] = term

    def positions(patch_col):
        patch = patch_col.astype(jnp.int32)
        which = lax.broadcasted_iota(jnp.int32, (patch.shape[0], 192), 1)
        want = jnp.where(which < 96, patch >> 5, patch & 31)
        return nn(hot((which & 31) == want), ptab[...])

    for i in (2, 3, 4):
        loads[i].wait()
    pair = pl.ds(pl.multiple_of((m // 2) * 128, 128), 128)
    odd = jnp.full((1024, HD), lax.rem(m, 2), jnp.int32) == 1
    for i, w in enumerate((wq, wk, wv)):
        two = w[:, pair].astype(F32)
        wh[:, i * HD : (i + 1) * HD] = jnp.where(odd, two[:, HD:], two[:, :HD]).astype(BF16)

    gain = gain_r[...]
    token = mask_r[...]

    def masked(i, _):
        s = fiota((256, 1024), 0) + (i * 256).astype(F32)
        order = jnp.sum(jnp.where(place_row == s, lane, 0.0), axis=1, keepdims=True)
        p = positions(order)
        pos[rows(i, 256), :] = p
        std, _ = norm(token + p)
        tab[rows(i, 256), :] = nn((std * gain).astype(BF16), wh[...])
        return 0

    lax.fori_loop(0, 4, masked, 0)
    encT[...] = jnp.transpose(enc[...])
    for b in range(2):
        xvis[b * 256 : (b + 1) * 256, :] = positions(viscol[b * 256 : (b + 1) * 256, :])

    mine = rows(m, 32)

    def add_part(j, total):
        k = lax.rem(m + j, N)
        wait_from(k, rsbuf.at[k], rs_s)
        return total + rsbuf[k].astype(F32)

    emb[mine, :] = lax.fori_loop(1, N, add_part, part[mine, :].astype(F32)).astype(BF16)
    wait_sends(part.at[rows(0, 32)])

    def send_emb(j, _):
        copy_to(lax.rem(m + j, N), emb.at[mine], emb.at[mine], ag_s.at[m]).start()
        return 0

    lax.fori_loop(1, N, send_emb, 0)

    def get_emb(j, _):
        k = lax.rem(m + j, N)
        wait_from(k, emb.at[rows(k, 32)], ag_s)
        return 0

    lax.fori_loop(1, N, get_emb, 0)
    wait_sends(emb.at[mine])

    def visible_rows(b, _):
        r = rows(b, 256)
        x = emb[r, :].astype(F32) + xvis[r, :]
        xvis[r, :] = x
        std, _ = norm(x)
        qkvv[r, :] = nn((std * gain).astype(BF16), wh[...]).astype(BF16)
        return 0

    lax.fori_loop(0, 2, visible_rows, 0)

    v2[...] = jnp.zeros_like(v2)

    for b in range(2):

        def place_rows(i, _, b=b):
            s = fiota((256, 256), 0) + (i * 256).astype(F32)
            put = jnp.where(vprow[b : b + 1, :] == s, 1.0, 0.0)
            seen = jnp.sum(put, axis=1, keepdims=True) > 0.0
            moved = nn(put.astype(BF16), qkvv[b * 256 : (b + 1) * 256, :])
            full = jnp.where(seen, moved, tab[rows(i, 256), :]).astype(BF16)
            qf[b, rows(i, 256), :] = full[:, 0:HD] * jnp.array(0.125, BF16)
            kf[b, rows(i, 256), :] = full[:, HD : 2 * HD]
            v2[b, rows(i, 256), b * HD : (b + 1) * HD] = full[:, 2 * HD :]
            return 0

        lax.fori_loop(0, 4, place_rows, 0)

    def attend(jj, _):
        g = lax.rem(my_group + jj, 4)
        r = rows(g, 256)
        total = jnp.zeros((256, 2 * HD), F32)
        for b in range(2):
            s = nt(qf[b, r, :], kf[b])
            top = jnp.max(s, axis=1, keepdims=True)
            e = jnp.exp(s - top)
            size = jnp.sum(e, axis=1, keepdims=True)
            lse[b, r, :] = top + jnp.log(size)
            total = total + nn((e * (1.0 / size)).astype(BF16), v2[b])
        attp[r, :] = total.astype(BF16)

        @pl.when(jj < 4)
        def _():
            for i in range(4):
                k = 4 * g + i
                copy_to(k, attp.at[rows(k, 64)], attb.at[m], at_s.at[m]).start()

        @pl.when(jj == 4)
        def _():
            for i in range(1, 4):
                k = 4 * g + lax.rem(m + i, 4)
                copy_to(k, attp.at[rows(k, 64)], attb.at[m], at_s.at[m]).start()

        return 0

    lax.fori_loop(1, 5, attend, 0)

    for i in (5, 6, 7):
        loads[i].wait()
    own_place = fiota((64, 256), 0) + (m * 64).astype(F32)
    own_pos = pos[rows(m, 64), :]
    seen_own, inputs = [], []
    for b in range(2):
        put = jnp.where(vprow[b : b + 1, :] == own_place, 1.0, 0.0)
        seen = jnp.sum(put, axis=1, keepdims=True) > 0.0
        moved = nn(put.astype(BF16), emb[b * 256 : (b + 1) * 256, :])
        inputs.append(jnp.where(seen, moved, token) + own_pos)
        seen_own.append(seen)
    inputs = jnp.concatenate(inputs, axis=0)

    attb[m] = attp[rows(m, 64), :]

    def get_att(j, _):
        k = lax.rem(m + j, N)
        wait_from(k, attb.at[k], at_s)
        return 0

    lax.fori_loop(1, N, get_att, 0)
    wait_sends(attp.at[rows(0, 64)])
    for h in range(N):
        for b in range(2):
            attf[b * 64 : (b + 1) * 64, h * HD : (h + 1) * HD] = attb[h, :, b * HD : (b + 1) * HD]

    updated = inputs + nn(attf[...], wo[...])
    pixels = nn(updated.astype(BF16), wp[...])
    resid = []
    for b in range(2):
        px = pixels[b * 64 : (b + 1) * 64, :]
        pred_o[b] = px.astype(BF16)
        resid.append(jnp.where(seen_own[b], 0.0, px - tgt[b].astype(F32)).astype(BF16))
    grad_up = nt(jnp.concatenate(resid, axis=0), wp[...]).astype(BF16)
    grad_att = nt(grad_up, wo[...]).astype(BF16)
    for h in range(N):
        for b in range(2):
            cut = slice(h * HD, (h + 1) * HD)
            gsend[h, :, b * HD : (b + 1) * HD] = grad_att[b * 64 : (b + 1) * 64, cut]
            gsend[h, :, (2 + b) * HD : (3 + b) * HD] = grad_up[b * 64 : (b + 1) * 64, cut]

    own64 = rows(m, 64)

    def send_grad(j, _):
        k = lax.rem(m + j, N)
        copy_to(k, gsend.at[k], gall.at[own64], g_s.at[m]).start()
        return 0

    lax.fori_loop(1, N, send_grad, 0)
    gall[own64, :] = gsend[m]

    def get_grad(j, _):
        k = lax.rem(m + j, N)
        wait_from(k, gall.at[rows(k, 64)], g_s)
        return 0

    lax.fori_loop(1, N, get_grad, 0)
    wait_sends(gsend.at[0])

    for b in range(2):
        r = slice(b * 256, (b + 1) * 256)
        cut = slice(b * HD, (b + 1) * HD)
        kv = qkvv[r, HD : 2 * HD]
        vv = qkvv[r, 2 * HD :]
        vfull = v2[b][:, cut]

        def keys_back(i, totals, b=b, cut=cut, kv=kv, vv=vv):
            q = rows(i, 256)
            g = gall[q, cut]
            delta = jnp.sum(g.astype(F32) * attp[q, cut].astype(F32), axis=1, keepdims=True)
            p = jnp.exp(nt(qf[b, q, :], kv) - lse[b, q, :])
            ds = (p * (nt(g, vv) - delta)).astype(BF16)
            return (totals[0] + tn(ds, qf[b, q, :]), totals[1] + tn(p.astype(BF16), g))

        nil = jnp.zeros((256, HD), F32)
        dk, dv = lax.fori_loop(0, 4, keys_back, (nil, nil))

        take = hot(vpcol[r, :] == lane)
        gv = nn(take, gall[...]).astype(BF16)
        av = nn(take, attp[...])[:, cut]
        s = nt(qkvv[r, 0:HD] * jnp.array(0.125, BF16), kf[b])
        e = jnp.exp(s - jnp.max(s, axis=1, keepdims=True))
        p = e * (1.0 / jnp.sum(e, axis=1, keepdims=True))
        delta = jnp.sum(gv[:, cut].astype(F32) * av, axis=1, keepdims=True)
        ds = (p * (nt(gv[:, cut], vfull) - delta)).astype(BF16)
        dq = nn(ds, kf[b]) * 0.125
        dpack[r, 0:HD] = dq.astype(BF16)
        dpack[r, HD : 2 * HD] = dk.astype(BF16)
        dpack[r, 2 * HD : 3 * HD] = dv.astype(BF16)
        dpack[r, 3 * HD :] = gv[:, (2 + b) * HD : (3 + b) * HD]

    def send_d(j, _):
        k = lax.rem(m + j, N)
        copy_to(k, dpack.at[rows(k, 32)], dbuf.at[m], d_s.at[m]).start()
        return 0

    lax.fori_loop(1, N, send_d, 0)
    dbuf[m] = dpack[mine, :]

    std, inv = norm(xvis[mine, :])

    def get_d(j, _):
        k = lax.rem(m + j, N)
        wait_from(k, dbuf.at[k], d_s)
        return 0

    lax.fori_loop(1, N, get_d, 0)
    wait_sends(dpack.at[rows(0, 32)])
    for h in range(N):
        for t in range(4):
            df[t, :, h * HD : (h + 1) * HD] = dbuf[h, :, t * HD : (t + 1) * HD]
    scaled = (nt(df[0], wq[...]) + nt(df[1], wk[...]) + nt(df[2], wv[...])) * gain
    back = df[3].astype(F32) + inv * (
        scaled
        - jnp.mean(scaled, axis=-1, keepdims=True)
        - std * jnp.mean(scaled * std, axis=-1, keepdims=True)
    )
    ret[mine, :] = back.astype(BF16)

    def send_ret(j, _):
        copy_to(lax.rem(m + j, N), ret.at[mine], ret.at[mine], ag2_s.at[m]).start()
        return 0

    lax.fori_loop(1, N, send_ret, 0)

    def get_ret(j, _):
        k = lax.rem(m + j, N)
        wait_from(k, ret.at[rows(k, 32)], ag2_s)
        return 0

    lax.fori_loop(1, N, get_ret, 0)
    wait_sends(ret.at[mine])

    def local_grad(i, _):
        both = nn(encT[...], ret[:, rows(i, 256)]).astype(BF16)
        loc[2 * i] = both[:, 0:128]
        loc[2 * i + 1] = both[:, 128:256]
        return 0

    lax.fori_loop(0, 4, local_grad, 0)
    my_half = rows(c, 192)
    other_half = rows(1 - c, 192)

    def cross(src, dst, i):
        return pltpu.make_async_remote_copy(
            src_ref=src, dst_ref=dst, send_sem=csend.at[i], recv_sem=crecv.at[i],
            device_id={"section": 1 - c}, device_id_type=MESH,
        )

    first = cross(loc.at[:, other_half], half_in, 0)
    first.start()

    def encoder_grad(i, _):
        encg_o[rows(i, 256), :] = nt(ret[rows(i, 256), :], we[...]).astype(BF16)
        return 0

    lax.fori_loop(0, 2, encoder_grad, 0)
    first.wait()

    def add_half(i, _):
        zin[i] = (loc[i, my_half, :].astype(F32) + half_in[i].astype(F32)).astype(BF16)
        return 0

    lax.fori_loop(0, NZ, add_half, 0)

    def z_copy(k, src, dst, recv):
        return pltpu.make_async_remote_copy(
            src_ref=src, dst_ref=dst, send_sem=zsend.at[k], recv_sem=recv,
            device_id={"dp": k}, device_id_type=MESH,
        )

    def send_z(j, _):
        k = lax.rem(z + j, NZ)
        z_copy(k, zin.at[k], zbuf.at[z], z1_s.at[z]).start()
        return 0

    lax.fori_loop(1, NZ, send_z, 0)

    def add_z(j, total):
        k = lax.rem(z + j, NZ)
        z_copy(k, zbuf.at[k], zbuf.at[k], z1_s.at[k]).wait_recv()
        return total + zbuf[k].astype(F32)

    zgat[z] = lax.fori_loop(1, NZ, add_z, zin[z].astype(F32)).astype(BF16)

    def wait_z(j, _):
        k = lax.rem(z + j, NZ)
        z_copy(k, zin.at[0], zin.at[0], zsend.at[k]).wait_send()
        return 0

    lax.fori_loop(1, NZ, wait_z, 0)

    def send_z2(j, _):
        k = lax.rem(z + j, NZ)
        z_copy(k, zgat.at[z], zgat.at[z], z2_s.at[z]).start()
        return 0

    lax.fori_loop(1, NZ, send_z2, 0)

    def get_z2(j, _):
        k = lax.rem(z + j, NZ)
        z_copy(k, zgat.at[k], zgat.at[k], z2_s.at[k]).wait_recv()
        return 0

    lax.fori_loop(1, NZ, get_z2, 0)
    second = cross(zgat, zown, 1)
    second.start()
    for i in range(NZ):
        emb_o[my_half, i * 128 : (i + 1) * 128] = zgat[i]
    second.wait()
    for i in range(NZ):
        emb_o[other_half, i * 128 : (i + 1) * 128] = zown[i]
    lax.fori_loop(1, NZ, wait_z, 0)


def body(
    encoded, visible, owner, embed_weight, mask_token, norm_gain,
    query_weight, key_weight, value_weight, out_weight, pixel_weight, targets,
):
    quarter = 256
    freqs = 10000.0 ** (-jnp.arange(quarter, dtype=F32) / quarter)
    angle = jnp.arange(GRID, dtype=F32)[:, None] * freqs[None, :]
    trig = jnp.concatenate([jnp.sin(angle), jnp.cos(angle)], axis=1)
    vm = pl.BlockSpec(memory_space=pltpu.VMEM)
    hbm = pl.BlockSpec(memory_space=pl.ANY)
    V = pltpu.VMEM
    dma = pltpu.SemaphoreType.DMA
    scratch = [
        V((512, 384), BF16), V((384, 1024), BF16),
        V((1024, 1024), BF16), V((1024, 1024), BF16), V((1024, 1024), BF16), V((1024, 1024), BF16),
        V((1024, 768), BF16), V((2, 64, 768), BF16),
        V((512, 1024), BF16), V((N, 32, 1024), BF16), V((512, 1024), BF16), V((384, 512), BF16),
        V((1024, 1), F32), V((2, 256), F32), V((512, 1), F32), V((512, 1), F32), V((192, 1024), BF16),
        V((1024, 1024), F32), V((512, 1024), F32), V((1024, 192), BF16), V((1024, 192), F32), V((512, 192), BF16),
        V((2, 1024, HD), BF16), V((2, 1024, HD), BF16), V((2, 1024, 2 * HD), BF16), V((2, 1024, 1), F32),
        V((1024, 128), BF16), V((N, 64, 128), BF16), V((128, 1024), BF16),
        V((N, 64, 256), BF16), V((1024, 256), BF16), V((512, 256), BF16), V((N, 32, 256), BF16),
        V((4, 32, 1024), BF16), V((512, 1024), BF16),
        V((NZ, 384, 128), BF16), V((NZ, 192, 128), BF16), V((NZ, 192, 128), BF16),
        V((NZ, 192, 128), BF16), V((NZ, 192, 128), BF16), V((NZ, 192, 128), BF16),
        dma((8,)), dma((N,)), dma((N,)), dma((N,)), dma((N,)), dma((N,)), dma((N,)), dma((N,)),
        dma((NZ,)), dma((NZ,)), dma((NZ,)), dma((2,)), dma((2,)),
    ]
    predicted, encoded_grad, summed = pl.pallas_call(
        kernel,
        out_shape=(
            jax.ShapeDtypeStruct((2, 64, 768), BF16),
            jax.ShapeDtypeStruct((512, 384), BF16),
            jax.ShapeDtypeStruct((384, 1024), BF16),
        ),
        in_specs=[hbm, hbm, vm, vm, vm, vm, hbm, hbm, hbm, hbm, hbm, hbm, vm],
        out_specs=(vm, vm, vm),
        scratch_shapes=scratch,
        compiler_params=pltpu.CompilerParams(
            collective_id=0, has_side_effects=True, vmem_limit_bytes=58 * 1024 * 1024
        ),
        cost_estimate=pl.CostEstimate(flops=8_000_000_000, bytes_accessed=16_000_000, transcendentals=4_000_000),
    )(
        encoded, embed_weight, owner.reshape(1, 1024), visible, mask_token.reshape(1, 1024), norm_gain.reshape(1, 1024),
        query_weight, key_weight, value_weight, out_weight, pixel_weight, targets, trig,
    )
    return predicted, encoded_grad, summed.astype(F32) * 8192 ** (-0.5)


def solution(mesh):
    placed = (
        P(("dp", "section"), "mp"),
        P(("dp", "section"), None),
        P(),
        P("mp", None),
        P(),
        P(),
        P(),
        P(),
        P(),
        P(),
        P(),
        P(("dp", "section"), "mp", None),
    )
    return jax.shard_map(
        body,
        mesh=mesh,
        in_specs=placed,
        out_specs=(P(("dp", "section"), "mp", None), P(("dp", "section"), "mp"), P("mp", None)),
        check_vma=False,
    )
```

time: 658 us -> 131 us (0.20)
  the two profiles are of different devices: /device:TPU:1 before, /device:TPU:3 now
where the time goes in v1:
time: 131 us
  Pallas kernels  126 us (96%)
  other arithmetic  3.31 us (3%)
  local copies, waits for them, and re-layouts  1.43 us (1%)
    pallas_call x1, Pallas kernels, body(): pl.pallas_call(kernel, out_shape=(jax.ShapeDtypeStruct((2, 64, 768), BF16...  126 us

profile of v1, /device:TPU:3, one launch (start us, length us, event | category | flops | bytes accessed | tf_op | source)
XLA Modules:
  0.0 131.0 jit_solution(12175354451675336968)
XLA Ops:
  0.6 0.1 fusion.1
  0.8 0.6 pad_maximum_fusion.trig_r
  1.4 125.6 %shard_map.139 = (bf16[2,64,768]{2,1,0:T(8,128)(2,1)}, bf16[512,384]{1,0:T(8,128)(2,1)}, bf16[384,1024]{1,0:T(8,128)(2,1)}) custom-call(bf16[512,384]{1,0:T(8,128)(2,1)} %enc_h.1, bf16[384,1024]{1,0:T(8,128)(2,1)} %we_h.1, s32[1,1024]{1,0:T(1,128)} %bitcast.3, s32[2,256]{1,0:T(2,128)} %vis_r.1, f32[1,1024]{1,0:T(1,128)} %bitcast.4, f32[1,1024]{1,0:T(1,128)} %bitcast.5, ...), custom_call_target="tpu_custom_call" | custom-call | flops 8000000000 | bytes 16000000 | tf_op jit(solution)/shard_map/pallas_call | solution.py:516
  127.0 0.0 copy-start.1
  127.0 0.0 copy-start
  127.0 2.5 %convert_multiply_fusion = f32[384,1024]{1,0:T(8,128)} fusion(bf16[384,1024]{1,0:T(8,128)(2,1)} %get-tuple-element.8), kind=kLoop, calls=%fused_computation | loop fusion | flops 786432 | bytes 2359296 | tf_op jit(solution)/shard_map/mul | solution.py:534
  129.5 0.0 copy-done.1
  129.5 0.7 copy.17
  130.2 0.0 copy-done
  130.2 0.7 copy.18
  (1 shorter events, 0.0 us)
Async XLA Ops:
  127.0 2.5 %copy-start.1 = (bf16[2,64,768]{2,1,0:T(8,128)(2,1)S(1)}, bf16[2,64,768]{2,1,0:T(8,128)(2,1)}, u32[]{:S(2)}) copy-start(bf16[2,64,768]{2,1,0:T(8,128)(2,1)} %get-tuple-element.14) | copy-start | bytes 589828
  127.0 3.2 %copy-start = (bf16[512,384]{1,0:T(8,128)(2,1)S(1)}, bf16[512,384]{1,0:T(8,128)(2,1)}, u32[]{:S(2)}) copy-start(bf16[512,384]{1,0:T(8,128)(2,1)} %get-tuple-element.15) | copy-start | bytes 1179652

commit v2 on v1

v2 whole, which is shorter than its diff:
```python
import functools

import jax
import jax.numpy as jnp
from jax import lax
from jax.experimental import pallas as pl
from jax.experimental.pallas import tpu as pltpu
from jax.sharding import PartitionSpec as P

MESH = pl.DeviceIdType.MESH
F32 = jnp.float32
BF16 = jnp.bfloat16
GRID = 32
N = 16
NZ = 8
HD = 64
PIECES = 2
WIDE = 1024 // PIECES
TILES = WIDE // 128
DEEP = 192 * TILES // NZ


def nn(a, b):
    return lax.dot_general(a, b, (((1,), (0,)), ((), ())), preferred_element_type=F32)


def nt(a, b):
    return lax.dot_general(a, b, (((1,), (1,)), ((), ())), preferred_element_type=F32)


def tn(a, b):
    return lax.dot_general(a, b, (((0,), (0,)), ((), ())), preferred_element_type=F32)


def fiota(shape, dim):
    return lax.broadcasted_iota(jnp.int32, shape, dim).astype(F32)


def hot(cond):
    return jnp.where(cond, 1.0, 0.0).astype(BF16)


def norm(x):
    c = x - jnp.mean(x, axis=-1, keepdims=True)
    inv = lax.rsqrt(jnp.mean(c * c, axis=-1, keepdims=True) + 1e-06)
    return c * inv, inv


def rows(i, size):
    return pl.ds(pl.multiple_of(i * size, size), size)


def kernel(
    enc_h, we_h, own_r, vis_r, mask_r, gain_r, wq_h, wk_h, wv_h, wo_h, wp_h, tgt_h, trig_r,
    pred_o, encg_o, emb_o,
    enc, we, wq, wk, wv, wo, wp, tgt,
    part, rsbuf, emb, encT,
    placec, vprow, vpcol, viscol, seenrow, seencol, put, take, ptab, pos, xvis, wh,
    qt, kt, vt, vt2, mt, lt, acc,
    qv, kv, vv, vv2, av2, p1s, p2s, ps,
    attp, attb, attf, gasend, gusend, gaall, guall, dpack, dbuf, df, ret,
    loc, half_in, zin, zbuf, zgat, zown,
    lsem, ssem, usem, rs_s, ag_s, at_s, ga_s, gu_s, d_s, ag2send, ag2_s, zsend, z1_s, z2send, z2_s,
    csend, crecv, fsend, frecv,
):
    m = lax.axis_index("mp")
    z = lax.axis_index("dp")
    c = lax.axis_index("section")

    pairs = [(enc_h, enc), (we_h, we), (wq_h, wq), (wk_h, wk), (wv_h, wv), (wo_h, wo), (wp_h, wp), (tgt_h, tgt)]
    loads = [pltpu.make_async_copy(s, d, lsem.at[i]) for i, (s, d) in enumerate(pairs)]
    for load in loads:
        load.start()

    barrier = pltpu.get_barrier_semaphore()

    def greet_mp(j, _):
        pl.semaphore_signal(barrier, inc=1, device_id={"mp": lax.rem(m + j, N)}, device_id_type=MESH)
        return 0

    def greet_z(j, _):
        pl.semaphore_signal(barrier, inc=1, device_id={"dp": lax.rem(z + j, NZ)}, device_id_type=MESH)
        return 0

    lax.fori_loop(1, N, greet_mp, 0)
    lax.fori_loop(1, NZ, greet_z, 0)
    pl.semaphore_signal(barrier, inc=1, device_id={"section": 1 - c}, device_id_type=MESH)

    def copy_to(k, src, dst, recv, send=ssem):
        return pltpu.make_async_remote_copy(
            src_ref=src, dst_ref=dst, send_sem=send.at[k], recv_sem=recv,
            device_id={"mp": k}, device_id_type=MESH,
        )

    def each_peer(f):
        def one(j, _):
            f(lax.rem(m + j, N))
            return 0

        lax.fori_loop(1, N, one, 0)

    def each_z(f):
        def one(j, _):
            f(lax.rem(z + j, NZ))
            return 0

        lax.fori_loop(1, NZ, one, 0)

    def wait_sends(src, send=ssem):
        each_peer(lambda k: copy_to(k, src, src, send.at[k], send).wait_send())

    def wait_from(k, dst, sems):
        copy_to(k, dst, dst, sems.at[k]).wait_recv()

    loads[0].wait()
    loads[1].wait()

    def partial_block(g):
        part[rows(g, 128), :] = nn(enc[rows(g, 128), :], we[...]).astype(BF16)

    def send_part(k):
        copy_to(k, part.at[rows(k, 32)], rsbuf.at[m], rs_s.at[m]).start()

    my_group = m // 4
    partial_block(lax.rem(my_group + 1, 4))
    pl.semaphore_wait(barrier, N - 1 + NZ - 1 + 1)

    def send_group(jj, _):
        g = lax.rem(my_group + jj, 4)

        @pl.when(jj > 1)
        def _():
            partial_block(g)

        for i in range(4):
            send_part(4 * g + i)
        return 0

    lax.fori_loop(1, 4, send_group, 0)
    partial_block(my_group)
    for i in range(1, 4):
        send_part(4 * my_group + lax.rem(m + i, 4))

    key_row = own_r[...].astype(F32) * 1024.0 + fiota((1, 1024), 1)
    lane = fiota((256, 1024), 1)

    def places(i, place_row):
        s = fiota((256, 1024), 0) + (i * 256).astype(F32)
        key_col = jnp.sum(jnp.where(lane == s, key_row, 0.0), axis=1, keepdims=True)
        less = jnp.where(key_row < key_col, 1.0, 0.0)
        placec[rows(i, 256), :] = jnp.sum(less, axis=1, keepdims=True)
        more = jnp.where(key_col < key_row, 1.0, 0.0)
        return place_row + jnp.sum(more, axis=0, keepdims=True)

    place_row = lax.fori_loop(0, 4, places, jnp.zeros((1, 1024), F32))

    for b in range(2):
        r = slice(b * 256, (b + 1) * 256)
        vrow = vis_r[b : b + 1, :].astype(F32)
        vcol = jnp.sum(jnp.where(fiota((256, 256), 0) == fiota((256, 256), 1), vrow, 0.0), axis=1, keepdims=True)
        viscol[r, :] = vcol
        vpcol[r, :] = jnp.sum(jnp.where(lane == vcol, place_row, 0.0), axis=1, keepdims=True)
        vprow[b : b + 1, :] = jnp.sum(
            jnp.where(fiota((1024, 256), 0) == vrow, placec[...], 0.0), axis=0, keepdims=True
        )
        gather = jnp.where(vpcol[r, :] == lane, 1.0, 0.0)
        seenrow[b : b + 1, :] = jnp.sum(gather, axis=0, keepdims=True)
        take[r, :] = gather.astype(BF16)
        spread = jnp.where(vprow[b : b + 1, :] == fiota((1024, 256), 0), 1.0, 0.0)
        seencol[b] = jnp.sum(spread, axis=1, keepdims=True)
        put[b] = spread.astype(BF16)

    trig = trig_r[...]
    hi = trig.astype(BF16)
    rest = trig - hi.astype(F32)
    mid = rest.astype(BF16)
    low = (rest - mid.astype(F32)).astype(BF16)
    ptab[...] = jnp.zeros_like(ptab)
    for i, term in enumerate((hi, mid, low)):
        ptab[32 * i : 32 * i + 32, 0:512] = term
        ptab[96 + 32 * i : 128 + 32 * i, 512:1024] = term

    def positions(patch_col):
        patch = patch_col.astype(jnp.int32)
        which = lax.broadcasted_iota(jnp.int32, (patch.shape[0], 192), 1)
        want = jnp.where(which < 96, patch >> 5, patch & 31)
        return nn(hot((which & 31) == want), ptab[...])

    for i in (2, 3, 4):
        loads[i].wait()
    pair = pl.ds(pl.multiple_of((m // 2) * 128, 128), 128)
    odd = jnp.full((1024, HD), lax.rem(m, 2), jnp.int32) == 1
    for i, w in enumerate((wq, wk, wv)):
        two = w[:, pair].astype(F32)
        wh[:, i * HD : (i + 1) * HD] = jnp.where(odd, two[:, HD:], two[:, :HD]).astype(BF16)

    gain = gain_r[...]
    token = mask_r[...]
    scale = jnp.array(0.125, BF16)

    vt2[...] = jnp.zeros_like(vt2)
    vv2[...] = jnp.zeros_like(vv2)

    def masked(i, _):
        r = rows(i, 256)
        s = fiota((256, 1024), 0) + (i * 256).astype(F32)
        order = jnp.sum(jnp.where(place_row == s, lane, 0.0), axis=1, keepdims=True)
        p = positions(order)
        pos[r, :] = p
        std, _ = norm(token + p)
        three = nn((std * gain).astype(BF16), wh[...]).astype(BF16)
        qt[r, :] = three[:, 0:HD] * scale
        kt[r, :] = three[:, HD : 2 * HD]
        vt[r, :] = three[:, 2 * HD :]
        for b in range(2):
            vt2[b, r, b * HD : (b + 1) * HD] = three[:, 2 * HD :]
        return 0

    lax.fori_loop(0, 4, masked, 0)
    for b in range(2):
        xvis[b * 256 : (b + 1) * 256, :] = positions(viscol[b * 256 : (b + 1) * 256, :])

    mine = rows(m, 32)

    def add_part(j, total):
        k = lax.rem(m + j, N)
        wait_from(k, rsbuf.at[k], rs_s)
        return total + rsbuf[k].astype(F32)

    emb[mine, :] = lax.fori_loop(1, N, add_part, part[mine, :].astype(F32)).astype(BF16)
    wait_sends(part.at[rows(0, 32)])
    each_peer(lambda k: copy_to(k, emb.at[mine], emb.at[mine], ag_s.at[m]).start())

    def table(i, _):
        r = rows(i, 256)
        s = nt(qt[r, :], kt[...])
        total = jnp.zeros((256, 2 * HD), F32)
        for b in range(2):
            held = jnp.where(seenrow[b : b + 1, :] > 0.0, -jnp.inf, s)
            top = jnp.max(held, axis=1, keepdims=True)
            e = jnp.exp(held - top)
            mt[b, r, :] = top
            lt[b, r, :] = jnp.sum(e, axis=1, keepdims=True)
            total = total + nn(e.astype(BF16), vt2[b])
        acc[r, :] = total
        return 0

    lax.fori_loop(0, 4, table, 0)
    encT[...] = jnp.transpose(enc[...])

    each_peer(lambda k: wait_from(k, emb.at[rows(k, 32)], ag_s))
    wait_sends(emb.at[mine])

    for b in range(2):
        r = slice(b * 256, (b + 1) * 256)
        x = emb[r, :].astype(F32) + xvis[r, :]
        xvis[r, :] = x
        std, _ = norm(x)
        three = nn((std * gain).astype(BF16), wh[...]).astype(BF16)
        q, k, v = three[:, 0:HD] * scale, three[:, HD : 2 * HD], three[:, 2 * HD :]
        qv[r, :] = q
        kv[r, :] = k
        vv[r, :] = v
        vv2[b, :, b * HD : (b + 1) * HD] = v
        s1 = jnp.where(seenrow[b : b + 1, :] > 0.0, -jnp.inf, nt(q, kt[...]))
        s2 = nt(q, k)
        top = jnp.maximum(jnp.max(s1, axis=1, keepdims=True), jnp.max(s2, axis=1, keepdims=True))
        e1 = jnp.exp(s1 - top)
        e2 = jnp.exp(s2 - top)
        inv = 1.0 / (jnp.sum(e1, axis=1, keepdims=True) + jnp.sum(e2, axis=1, keepdims=True))
        p1 = e1 * inv
        p2 = e2 * inv
        p1s[b] = p1
        p2s[b] = p2
        av2[b] = (nn(p1.astype(BF16), vt2[b]) + nn(p2.astype(BF16), vv2[b])).astype(BF16)

    left = lax.broadcasted_iota(jnp.int32, (256, 2 * HD), 1) < HD

    def attend(jj, _):
        g = lax.rem(my_group + jj, 4)
        r = rows(g, 256)
        added = jnp.zeros((256, 2 * HD), F32)
        placed = jnp.zeros((256, 2 * HD), F32)
        factor = []
        for b in range(2):
            s = nt(qt[r, :], kv[b * 256 : (b + 1) * 256, :])
            old = mt[b, r, :]
            top = jnp.maximum(old, jnp.max(s, axis=1, keepdims=True))
            e = jnp.exp(s - top)
            alpha = jnp.exp(old - top)
            inv = 1.0 / (alpha * lt[b, r, :] + jnp.sum(e, axis=1, keepdims=True))
            p = e * inv
            ps[b, r, :] = p
            factor.append(alpha * inv)
            added = added + nn(p.astype(BF16), vv2[b])
            placed = placed + nn(put[b, r, :], av2[b])
        att = acc[r, :] * jnp.where(left, factor[0], factor[1]) + added
        seen = jnp.where(left, seencol[0, r, :], seencol[1, r, :]) > 0.0
        attp[r, :] = jnp.where(seen, placed, att).astype(BF16)

        @pl.when(jj < 4)
        def _():
            for i in range(4):
                k = 4 * g + i
                copy_to(k, attp.at[rows(k, 64)], attb.at[m], at_s.at[m]).start()

        @pl.when(jj == 4)
        def _():
            for i in range(1, 4):
                k = 4 * g + lax.rem(m + i, 4)
                copy_to(k, attp.at[rows(k, 64)], attb.at[m], at_s.at[m]).start()

        return 0

    lax.fori_loop(1, 5, attend, 0)

    for i in (5, 6, 7):
        loads[i].wait()
    own64 = rows(m, 64)
    own_pos = pos[own64, :]
    seen_own, inputs = [], []
    for b in range(2):
        seen = seencol[b, own64, :] > 0.0
        moved = nn(put[b, own64, :], emb[b * 256 : (b + 1) * 256, :])
        inputs.append(jnp.where(seen, moved, token) + own_pos)
        seen_own.append(seen)
    inputs = jnp.concatenate(inputs, axis=0)

    attb[m] = attp[own64, :]
    each_peer(lambda k: wait_from(k, attb.at[k], at_s))
    wait_sends(attp.at[rows(0, 64)])
    for h in range(N):
        for b in range(2):
            attf[b * 64 : (b + 1) * 64, h * HD : (h + 1) * HD] = attb[h, :, b * HD : (b + 1) * HD]

    updated = inputs + nn(attf[...], wo[...])
    pixels = nn(updated.astype(BF16), wp[...])
    resid = []
    for b in range(2):
        px = pixels[b * 64 : (b + 1) * 64, :]
        pred_o[b] = px.astype(BF16)
        resid.append(jnp.where(seen_own[b], 0.0, px - tgt[b].astype(F32)).astype(BF16))
    grad_up = nt(jnp.concatenate(resid, axis=0), wp[...]).astype(BF16)
    grad_att = nt(grad_up, wo[...]).astype(BF16)
    for h in range(N):
        cut = slice(h * HD, (h + 1) * HD)
        for b in range(2):
            gasend[h, :, b * HD : (b + 1) * HD] = grad_att[b * 64 : (b + 1) * 64, cut]
    each_peer(lambda k: copy_to(k, gasend.at[k], gaall.at[own64], ga_s.at[m]).start())
    for h in range(N):
        cut = slice(h * HD, (h + 1) * HD)
        for b in range(2):
            gusend[h, :, b * HD : (b + 1) * HD] = grad_up[b * 64 : (b + 1) * 64, cut]
    each_peer(lambda k: copy_to(k, gusend.at[k], guall.at[own64], gu_s.at[m], usem).start())
    gaall[own64, :] = gasend[m]
    guall[own64, :] = gusend[m]
    each_peer(lambda k: wait_from(k, gaall.at[rows(k, 64)], ga_s))
    wait_sends(gasend.at[0])

    for b in range(2):
        r = slice(b * 256, (b + 1) * 256)
        cut = slice(b * HD, (b + 1) * HD)

        def keys_back(i, totals, b=b, r=r, cut=cut):
            q = rows(i, 256)
            wide = jnp.where(seencol[b, q, :] > 0.0, 0.0, gaall[q, cut].astype(F32))
            g = wide.astype(BF16)
            delta = jnp.sum(wide * attp[q, cut].astype(F32), axis=1, keepdims=True)
            p = ps[b, q, :]
            ds = (p * (nt(g, vv[r, :]) - delta)).astype(BF16)
            return (totals[0] + tn(ds, qt[q, :]), totals[1] + tn(p.astype(BF16), g))

        nil = jnp.zeros((256, HD), F32)
        dk, dv = lax.fori_loop(0, 4, keys_back, (nil, nil))

        gv = nn(take[r, :], gaall[...])[:, cut]
        delta = jnp.sum(gv * av2[b].astype(F32)[:, cut], axis=1, keepdims=True)
        gv = gv.astype(BF16)
        p2 = p2s[b]
        ds1 = (p1s[b] * (nt(gv, vt[...]) - delta)).astype(BF16)
        ds2 = (p2 * (nt(gv, vv[r, :]) - delta)).astype(BF16)
        dq = (nn(ds1, kt[...]) + nn(ds2, kv[r, :])) * 0.125
        dk = dk + tn(ds2, qv[r, :])
        dv = dv + tn(p2.astype(BF16), gv)
        dpack[r, 0:HD] = dq.astype(BF16)
        dpack[r, HD : 2 * HD] = dk.astype(BF16)
        dpack[r, 2 * HD : 3 * HD] = dv.astype(BF16)

    each_peer(lambda k: wait_from(k, guall.at[rows(k, 64)], gu_s))
    wait_sends(gusend.at[0], usem)
    for b in range(2):
        r = slice(b * 256, (b + 1) * 256)
        dpack[r, 3 * HD :] = nn(take[r, :], guall[...])[:, b * HD : (b + 1) * HD].astype(BF16)

    each_peer(lambda k: copy_to(k, dpack.at[rows(k, 32)], dbuf.at[m], d_s.at[m]).start())
    dbuf[m] = dpack[mine, :]

    std, inv = norm(xvis[mine, :])
    each_peer(lambda k: wait_from(k, dbuf.at[k], d_s))
    for h in range(N):
        for t in range(4):
            df[t, :, h * HD : (h + 1) * HD] = dbuf[h, :, t * HD : (t + 1) * HD]
    scaled = (nt(df[0], wq[...]) + nt(df[1], wk[...]) + nt(df[2], wv[...])) * gain
    back = df[3].astype(F32) + inv * (
        scaled
        - jnp.mean(scaled, axis=-1, keepdims=True)
        - std * jnp.mean(scaled * std, axis=-1, keepdims=True)
    )
    for q in range(PIECES):
        ret[q, mine, :] = back[:, q * WIDE : (q + 1) * WIDE].astype(BF16)

    def ret_copy(q, k, block):
        return copy_to(k, block, block, ag2_s.at[q, m], ag2send.at[q])

    for q in range(PIECES):
        each_peer(lambda k, q=q: ret_copy(q, k, ret.at[q, mine]).start())
    wait_sends(dpack.at[rows(0, 32)])

    def cross(src, dst, send, recv):
        return pltpu.make_async_remote_copy(
            src_ref=src, dst_ref=dst, send_sem=send, recv_sem=recv,
            device_id={"section": 1 - c}, device_id_type=MESH,
        )

    def z_copy(k, src, dst, send, recv):
        return pltpu.make_async_remote_copy(
            src_ref=src, dst_ref=dst, send_sem=send, recv_sem=recv,
            device_id={"dp": k}, device_id_type=MESH,
        )

    firsts = [cross(loc.at[q, :, rows(1 - c, 192)], half_in.at[q], csend.at[q], crecv.at[q]) for q in range(PIECES)]
    for q in range(PIECES):

        def get_ret(k, q=q):
            block = ret.at[q, rows(k, 32)]
            copy_to(k, block, block, ag2_s.at[q, k], ag2send.at[q]).wait_recv()

        each_peer(get_ret)
        both = nn(encT[...], ret[q]).astype(BF16)
        for t in range(TILES):
            loc[q, t] = both[:, t * 128 : (t + 1) * 128]
        firsts[q].start()

    def scatter_z(q):
        firsts[q].wait_recv()
        for d in range(NZ):
            own_part = loc[q, d % TILES, pl.ds(pl.multiple_of(c * 192 + (d // TILES) * DEEP, DEEP), DEEP), :]
            other = half_in[q, d % TILES, (d // TILES) * DEEP : (d // TILES + 1) * DEEP, :]
            zin[q, d] = (own_part.astype(F32) + other.astype(F32)).astype(BF16)
        each_z(lambda k: z_copy(k, zin.at[q, k], zbuf.at[q, z], zsend.at[q, k], z1_s.at[q, z]).start())

    for q in range(PIECES):
        scatter_z(q)
    forward = lambda q, k: cross(zgat.at[q, k], zown.at[q, k], fsend.at[q, k], frecv.at[q, k])
    for q in range(PIECES):

        def add_z(j, total, q=q):
            k = lax.rem(z + j, NZ)
            z_copy(k, zbuf.at[q, k], zbuf.at[q, k], zsend.at[q, k], z1_s.at[q, k]).wait_recv()
            return total + zbuf[q, k].astype(F32)

        zgat[q, z] = lax.fori_loop(1, NZ, add_z, zin[q, z].astype(F32)).astype(BF16)
        each_z(lambda k, q=q: z_copy(k, zgat.at[q, z], zgat.at[q, z], z2send.at[q, k], z2_s.at[q, z]).start())
        forward(q, z).start()

    def encoder_grad(i, _):
        r = rows(i, 256)
        total = nt(ret[0, r, :], we[:, 0:WIDE])
        for q in range(1, PIECES):
            total = total + nt(ret[q, r, :], we[:, q * WIDE : (q + 1) * WIDE])
        encg_o[r, :] = total.astype(BF16)
        return 0

    lax.fori_loop(0, 2, encoder_grad, 0)

    def get_z(q, k):
        z_copy(k, zgat.at[q, k], zgat.at[q, k], z2send.at[q, k], z2_s.at[q, k]).wait_recv()
        forward(q, k).start()

    shrink = 8192 ** (-0.5)

    def write(q, core, block):
        for d in range(NZ):
            at = pl.ds(pl.multiple_of(core * 192 + (d // TILES) * DEEP, DEEP), DEEP)
            lanes = q * WIDE + (d % TILES) * 128
            emb_o[at, lanes : lanes + 128] = block[q, d].astype(F32) * shrink

    for q in range(PIECES):
        each_z(lambda k, q=q: get_z(q, k))
        write(q, c, zgat)
    for q in range(PIECES):
        for k in range(NZ):
            forward(q, k).wait_recv()
        write(q, 1 - c, zown)

    for q in range(PIECES):
        each_peer(lambda k, q=q: ret_copy(q, k, ret.at[q, mine]).wait_send())
        firsts[q].wait_send()
        each_z(lambda k, q=q: z_copy(k, zin.at[q, k], zbuf.at[q, z], zsend.at[q, k], z1_s.at[q, z]).wait_send())
        each_z(lambda k, q=q: z_copy(k, zgat.at[q, z], zgat.at[q, z], z2send.at[q, k], z2_s.at[q, z]).wait_send())
        for k in range(NZ):
            forward(q, k).wait_send()


def body(
    encoded, visible, owner, embed_weight, mask_token, norm_gain,
    query_weight, key_weight, value_weight, out_weight, pixel_weight, targets,
):
    quarter = 256
    freqs = 10000.0 ** (-jnp.arange(quarter, dtype=F32) / quarter)
    angle = jnp.arange(GRID, dtype=F32)[:, None] * freqs[None, :]
    trig = jnp.concatenate([jnp.sin(angle), jnp.cos(angle)], axis=1)
    vm = pl.BlockSpec(memory_space=pltpu.VMEM)
    hbm = pl.BlockSpec(memory_space=pl.ANY)
    V = pltpu.VMEM
    dma = pltpu.SemaphoreType.DMA
    scratch = [
        V((512, 384), BF16), V((384, 1024), BF16),
        V((1024, 1024), BF16), V((1024, 1024), BF16), V((1024, 1024), BF16), V((1024, 1024), BF16),
        V((1024, 768), BF16), V((2, 64, 768), BF16),
        V((512, 1024), BF16), V((N, 32, 1024), BF16), V((512, 1024), BF16), V((384, 512), BF16),
        V((1024, 1), F32), V((2, 256), F32), V((512, 1), F32), V((512, 1), F32), V((2, 1024), F32), V((2, 1024, 1), F32),
        V((2, 1024, 256), BF16), V((512, 1024), BF16), V((192, 1024), BF16),
        V((1024, 1024), F32), V((512, 1024), F32), V((1024, 192), BF16),
        V((1024, HD), BF16), V((1024, HD), BF16), V((1024, HD), BF16), V((2, 1024, 2 * HD), BF16),
        V((2, 1024, 1), F32), V((2, 1024, 1), F32), V((1024, 2 * HD), F32),
        V((512, HD), BF16), V((512, HD), BF16), V((512, HD), BF16), V((2, 256, 2 * HD), BF16), V((2, 256, 2 * HD), BF16),
        V((2, 256, 1024), F32), V((2, 256, 256), F32), V((2, 1024, 256), F32),
        V((1024, 128), BF16), V((N, 64, 128), BF16), V((128, 1024), BF16),
        V((N, 64, 128), BF16), V((N, 64, 128), BF16), V((1024, 128), BF16), V((1024, 128), BF16),
        V((512, 256), BF16), V((N, 32, 256), BF16), V((4, 32, 1024), BF16), V((PIECES, 512, WIDE), BF16),
        V((PIECES, TILES, 384, 128), BF16), V((PIECES, TILES, 192, 128), BF16),
        V((PIECES, NZ, DEEP, 128), BF16), V((PIECES, NZ, DEEP, 128), BF16),
        V((PIECES, NZ, DEEP, 128), BF16), V((PIECES, NZ, DEEP, 128), BF16),
        dma((8,)), dma((N,)), dma((N,)), dma((N,)), dma((N,)), dma((N,)), dma((N,)), dma((N,)), dma((N,)),
        dma((PIECES, N)), dma((PIECES, N)), dma((PIECES, NZ)), dma((PIECES, NZ)), dma((PIECES, NZ)), dma((PIECES, NZ)),
        dma((PIECES,)), dma((PIECES,)), dma((PIECES, NZ)), dma((PIECES, NZ)),
    ]
    return pl.pallas_call(
        kernel,
        out_shape=(
            jax.ShapeDtypeStruct((2, 64, 768), BF16),
            jax.ShapeDtypeStruct((512, 384), BF16),
            jax.ShapeDtypeStruct((384, 1024), F32),
        ),
        in_specs=[hbm, hbm, vm, vm, vm, vm, hbm, hbm, hbm, hbm, hbm, hbm, vm],
        out_specs=(vm, vm, vm),
        scratch_shapes=scratch,
        compiler_params=pltpu.CompilerParams(
            collective_id=0, has_side_effects=True, vmem_limit_bytes=58 * 1024 * 1024
        ),
        cost_estimate=pl.CostEstimate(flops=8_000_000_000, bytes_accessed=16_000_000, transcendentals=4_000_000),
    )(
        encoded, embed_weight, owner.reshape(1, 1024), visible, mask_token.reshape(1, 1024), norm_gain.reshape(1, 1024),
        query_weight, key_weight, value_weight, out_weight, pixel_weight, targets, trig,
    )


def solution(mesh):
    placed = (
        P(("dp", "section"), "mp"),
        P(("dp", "section"), None),
        P(),
        P("mp", None),
        P(),
        P(),
        P(),
        P(),
        P(),
        P(),
        P(),
        P(("dp", "section"), "mp", None),
    )
    return jax.shard_map(
        body,
        mesh=mesh,
        in_specs=placed,
        out_specs=(P(("dp", "section"), "mp", None), P(("dp", "section"), "mp"), P("mp", None)),
        check_vma=False,
    )
```

time: 131 us -> 125 us (0.954)
  the two profiles are of different devices: /device:TPU:3 before, /device:TPU:1 now
where the time goes in v2:
time: 125 us
  Pallas kernels  118 us (94%)
  local copies, waits for them, and re-layouts  6.12 us (5%)
    pallas_call x1, Pallas kernels, body(): pl.pallas_call(kernel, out_shape=(jax.ShapeDtypeStruct((2, 64, 768), BF16...  118 us
    unnamed x3, local copies, waits for them, and re-layouts  6.12 us

profile of v2, /device:TPU:1, one launch (start us, length us, event | category | flops | bytes accessed | tf_op | source)
XLA Modules:
  0.0 125.2 jit_solution(5984487127118670291)
XLA Ops:
  0.6 0.1 fusion.1
  0.8 0.6 pad_maximum_fusion.trig_r
  1.4 117.6 %shard_map.139 = (bf16[2,64,768]{2,1,0:T(8,128)(2,1)}, bf16[512,384]{1,0:T(8,128)(2,1)}, f32[384,1024]{1,0:T(8,128)}) custom-call(bf16[512,384]{1,0:T(8,128)(2,1)} %enc_h.1, bf16[384,1024]{1,0:T(8,128)(2,1)} %we_h.1, s32[1,1024]{1,0:T(1,128)} %bitcast.3, s32[2,256]{1,0:T(2,128)} %vis_r.1, f32[1,1024]{1,0:T(1,128)} %bitcast.4, f32[1,1024]{1,0:T(1,128)} %bitcast.5, ...), custom_call_target="tpu_custom_call" | custom-call | flops 8000000000 | bytes 16000000 | tf_op jit(solution)/shard_map/pallas_call | solution.py:539
  119.0 1.6 %copy.18 = bf16[2,64,768]{2,1,0:T(8,128)(2,1)} copy(bf16[2,64,768]{2,1,0:T(8,128)(2,1)} %get-tuple-element.8) | data formatting | bytes 393216
  120.6 1.8 %copy.19 = bf16[512,384]{1,0:T(8,128)(2,1)} copy(bf16[512,384]{1,0:T(8,128)(2,1)} %get-tuple-element.9) | data formatting | bytes 786432
  122.4 2.7 %copy.20 = f32[384,1024]{1,0:T(8,128)} copy(f32[384,1024]{1,0:T(8,128)} %get-tuple-element.10) | data formatting | bytes 3145728
  (1 shorter events, 0.0 us)

commit v3 on v2

v3 whole, which is shorter than its diff:
```python
import functools

import jax
import jax.numpy as jnp
from jax import lax
from jax.experimental import pallas as pl
from jax.experimental.pallas import tpu as pltpu
from jax.sharding import PartitionSpec as P

MESH = pl.DeviceIdType.MESH
F32 = jnp.float32
BF16 = jnp.bfloat16
GRID = 32
N = 16
NZ = 8
HD = 64
PIECES = 2
WIDE = 1024 // PIECES
TILES = WIDE // 128
DEEP = 192 * TILES // NZ


def nn(a, b):
    return lax.dot_general(a, b, (((1,), (0,)), ((), ())), preferred_element_type=F32)


def nt(a, b):
    return lax.dot_general(a, b, (((1,), (1,)), ((), ())), preferred_element_type=F32)


def tn(a, b):
    return lax.dot_general(a, b, (((0,), (0,)), ((), ())), preferred_element_type=F32)


def fiota(shape, dim):
    return lax.broadcasted_iota(jnp.int32, shape, dim).astype(F32)


def hot(cond):
    return jnp.where(cond, 1.0, 0.0).astype(BF16)


def norm(x):
    c = x - jnp.mean(x, axis=-1, keepdims=True)
    inv = lax.rsqrt(jnp.mean(c * c, axis=-1, keepdims=True) + 1e-06)
    return c * inv, inv


def lanes(i, size):
    return pl.ds(pl.multiple_of(i * size, size), size)


def loop(n, f):
    def one(i, _):
        f(i)
        return 0

    lax.fori_loop(0, n, one, 0)


def rows(i, size):
    return pl.ds(pl.multiple_of(i * size, size), size)


def kernel(
    enc_h, we_h, own_r, vis_r, mask_r, gain_r, wq_h, wk_h, wv_h, wo_h, wp_h, tgt_h, trig_r,
    pred_o, encg_o, emb_o,
    enc, we, wq, wk, wv, wo, wp, tgt,
    part, rsbuf, encT,
    placec, viscol, seenrow, seencol, put, take, ptab, pos, xown, stdo, invo, wh,
    qt, kt, vt, mt, lt, acc,
    normed, fs, qsend, qall, av, ave, p1s, p2s, ps,
    attp, attb, attf, ef, updb, resid, gub, gab, gsend, gall, dpack, dbuf, df, sc, ret,
    loc, half_in, zin, zbuf, zgat, zown,
    lsem, send_s, recv_s, ag2send, ag2_s, zsend, z1_s, z2send, z2_s, csend, crecv, fsend, frecv,
):
    m = lax.axis_index("mp")
    z = lax.axis_index("dp")
    c = lax.axis_index("section")

    pairs = [(enc_h, enc), (we_h, we), (wq_h, wq), (wk_h, wk), (wv_h, wv), (wo_h, wo), (wp_h, wp), (tgt_h, tgt)]
    loads = [pltpu.make_async_copy(s, d, lsem.at[i]) for i, (s, d) in enumerate(pairs)]
    for load in loads:
        load.start()

    barrier = pltpu.get_barrier_semaphore()

    def each_peer(f):
        def one(j, _):
            f(lax.rem(m + j, N))
            return 0

        lax.fori_loop(1, N, one, 0)

    def each_z(f):
        def one(j, _):
            f(lax.rem(z + j, NZ))
            return 0

        lax.fori_loop(1, NZ, one, 0)

    each_peer(lambda k: pl.semaphore_signal(barrier, inc=1, device_id={"mp": k}, device_id_type=MESH))
    each_z(lambda k: pl.semaphore_signal(barrier, inc=1, device_id={"dp": k}, device_id_type=MESH))
    pl.semaphore_signal(barrier, inc=1, device_id={"section": 1 - c}, device_id_type=MESH)

    def to(k, src, dst, send, recv):
        return pltpu.make_async_remote_copy(
            src_ref=src, dst_ref=dst, send_sem=send, recv_sem=recv, device_id={"mp": k}, device_id_type=MESH
        )

    other = lax.rem(m + 1, N)

    def arrived(fifteen, sem):
        to(other, fifteen, fifteen, sem, sem).wait_recv()

    def left_here(fifteen, sem):
        to(other, fifteen, fifteen, sem, sem).wait_send()

    mine = rows(m, 16)
    own64 = rows(m, 64)

    loads[0].wait()
    loads[1].wait()

    def partial_block(g):
        both = jnp.concatenate(
            [enc[rows(g, 64), :], enc[pl.ds(pl.multiple_of(256 + g * 64, 64), 64), :]], axis=0
        )
        out = nn(both, we[...]).astype(BF16)
        part[0, rows(g, 64), :] = out[:64]
        part[1, rows(g, 64), :] = out[64:]

    loop(4, partial_block)
    pl.semaphore_wait(barrier, N - 1 + NZ - 1 + 1)
    each_peer(lambda k: to(k, part.at[:, rows(k, 16)], rsbuf.at[m], send_s.at[0], recv_s.at[0]).start())

    key_row = own_r[...].astype(F32) * 1024.0 + fiota((1, 1024), 1)
    lane = fiota((256, 1024), 1)

    def places(i, place_row):
        s = fiota((256, 1024), 0) + (i * 256).astype(F32)
        key_col = jnp.sum(jnp.where(lane == s, key_row, 0.0), axis=1, keepdims=True)
        less = jnp.where(key_row < key_col, 1.0, 0.0)
        placec[rows(i, 256), :] = jnp.sum(less, axis=1, keepdims=True)
        more = jnp.where(key_col < key_row, 1.0, 0.0)
        return place_row + jnp.sum(more, axis=0, keepdims=True)

    place_row = lax.fori_loop(0, 4, places, jnp.zeros((1, 1024), F32))

    def visible_places(b):
        vrow = vis_r[b].astype(F32)
        vcol = jnp.sum(jnp.where(fiota((256, 256), 0) == fiota((256, 256), 1), vrow, 0.0), axis=1, keepdims=True)
        viscol[b] = vcol
        vpc = jnp.sum(jnp.where(lane == vcol, place_row, 0.0), axis=1, keepdims=True)
        vpr = jnp.sum(jnp.where(fiota((1024, 256), 0) == vrow, placec[...], 0.0), axis=0, keepdims=True)
        gather = jnp.where(vpc == lane, 1.0, 0.0)
        seenrow[b] = jnp.sum(gather, axis=0, keepdims=True)
        take[b] = gather.astype(BF16)
        spread = jnp.where(vpr == fiota((1024, 256), 0), 1.0, 0.0)
        seencol[b] = jnp.sum(spread, axis=1, keepdims=True)
        put[b] = spread.astype(BF16)

    loop(2, visible_places)

    trig = trig_r[...]
    hi = trig.astype(BF16)
    rest = trig - hi.astype(F32)
    mid = rest.astype(BF16)
    low = (rest - mid.astype(F32)).astype(BF16)
    ptab[...] = jnp.zeros_like(ptab)
    for i, term in enumerate((hi, mid, low)):
        ptab[32 * i : 32 * i + 32, 0:512] = term
        ptab[96 + 32 * i : 128 + 32 * i, 512:1024] = term

    def positions(patch_col):
        patch = patch_col.astype(jnp.int32)
        which = lax.broadcasted_iota(jnp.int32, (patch.shape[0], 192), 1)
        want = jnp.where(which < 96, patch >> 5, patch & 31)
        return nn(hot((which & 31) == want), ptab[...])

    for i in (2, 3, 4):
        loads[i].wait()
    pair = lanes(m // 2, 128)
    odd = jnp.full((1024, HD), lax.rem(m, 2), jnp.int32) == 1
    for i, w in enumerate((wq, wk, wv)):
        two = w[:, pair].astype(F32)
        wh[:, i * HD : (i + 1) * HD] = jnp.where(odd, two[:, HD:], two[:, :HD]).astype(BF16)

    gain = gain_r[...]
    token = mask_r[...]
    scale = jnp.array(0.125, BF16)

    def masked(i):
        r = rows(i, 256)
        s = fiota((256, 1024), 0) + (i * 256).astype(F32)
        order = jnp.sum(jnp.where(place_row == s, lane, 0.0), axis=1, keepdims=True)
        p = positions(order)
        pos[r, :] = p
        std, _ = norm(token + p)
        three = nn((std * gain).astype(BF16), wh[...]).astype(BF16)
        qt[r, :] = three[:, 0:HD] * scale
        kt[r, :] = three[:, HD : 2 * HD]
        vt[r, :] = three[:, 2 * HD :]

    loop(4, masked)
    xown[...] = positions(jnp.concatenate([viscol[0, mine, :], viscol[1, mine, :]], axis=0))

    arrived(rsbuf.at[pl.ds(0, N - 1)], recv_s.at[0])
    rsbuf[m] = part[:, mine, :]
    own_rows = lax.fori_loop(
        0, N, lambda k, total: total + rsbuf[k].astype(F32), jnp.zeros((2, 16, 1024), F32)
    ).reshape(32, 1024)
    std, inv = norm(own_rows + xown[...])
    stdo[...] = std
    invo[...] = inv
    normed[...] = (std * gain).astype(BF16)
    fs[3] = own_rows.astype(BF16)

    def project(i):
        cut = lanes(i, 256)
        fs[0, :, cut] = nn(normed[...], wq[:, cut]).astype(BF16) * scale
        fs[1, :, cut] = nn(normed[...], wk[:, cut]).astype(BF16)
        fs[2, :, cut] = nn(normed[...], wv[:, cut]).astype(BF16)

    loop(4, project)

    def pack_rows(i):
        for t in range(4):
            two = fs[t, :, lanes(i, 128)].reshape(2, 16, 128)
            qsend[2 * i, :, :, t * HD : (t + 1) * HD] = two[:, :, :HD]
            qsend[2 * i + 1, :, :, t * HD : (t + 1) * HD] = two[:, :, HD:]

    loop(N // 2, pack_rows)
    each_peer(lambda k: to(k, qsend.at[k], qall.at[:, mine], send_s.at[1], recv_s.at[1]).start())
    qall[:, mine, :] = qsend[m]

    def table(i):
        r = rows(i, 256)
        s = nt(qt[r, :], kt[...])
        for b in range(2):
            held = jnp.where(seenrow[b] > 0.0, -jnp.inf, s)
            top = jnp.max(held, axis=1, keepdims=True)
            e = jnp.exp(held - top)
            mt[b, r, :] = top
            lt[b, r, :] = jnp.sum(e, axis=1, keepdims=True)
            acc[b, r, :] = nn(e.astype(BF16), vt[...])

    loop(4, table)
    encT[...] = jnp.transpose(enc[...])

    arrived(qall.at[:, pl.ds(0, 240)], recv_s.at[1])

    my_group = m // 4

    def attention(b):
        q, k, v = (qall[b, :, t * HD : (t + 1) * HD] for t in range(3))
        s1 = jnp.where(seenrow[b] > 0.0, -jnp.inf, nt(q, kt[...]))
        s2 = nt(q, k)
        top = jnp.maximum(jnp.max(s1, axis=1, keepdims=True), jnp.max(s2, axis=1, keepdims=True))
        e1 = jnp.exp(s1 - top)
        e2 = jnp.exp(s2 - top)
        inv = 1.0 / (jnp.sum(e1, axis=1, keepdims=True) + jnp.sum(e2, axis=1, keepdims=True))
        p1 = e1 * inv
        p2 = e2 * inv
        p1s[b] = p1
        p2s[b] = p2
        a = (nn(p1.astype(BF16), vt[...]) + nn(p2.astype(BF16), v)).astype(BF16)
        av[b] = a
        ave[b, :, 0:HD] = a
        ave[b, :, HD:] = qall[b, :, 3 * HD :]

        def attend(jj, _):
            g = lax.rem(my_group + jj, 4)
            r = rows(g, 256)
            s = nt(qt[r, :], qall[b, :, HD : 2 * HD])
            old = mt[b, r, :]
            top = jnp.maximum(old, jnp.max(s, axis=1, keepdims=True))
            e = jnp.exp(s - top)
            alpha = jnp.exp(old - top)
            inv = 1.0 / (alpha * lt[b, r, :] + jnp.sum(e, axis=1, keepdims=True))
            p = e * inv
            ps[b, r, :] = p
            att = acc[b, r, :] * (alpha * inv) + nn(p.astype(BF16), qall[b, :, 2 * HD : 3 * HD])
            placed = nn(put[b, r, :], ave[b])
            att = jnp.where(seencol[b, r, :] > 0.0, placed[:, 0:HD], att)
            attp[b, r, 0:HD] = att.astype(BF16)
            attp[b, r, HD:] = placed[:, HD:].astype(BF16)

            def send(i, _):
                k = 4 * g + lax.rem(m + i, 4)
                to(k, attp.at[b, rows(k, 64)], attb.at[b, m], send_s.at[2 + b], recv_s.at[2 + b]).start()
                return 0

            lax.fori_loop(jnp.where(jj == 4, 1, 0), 4, send, 0)
            return 0

        lax.fori_loop(1, 5, attend, 0)
        attb[b, m] = attp[b, own64, :]

    loop(2, attention)

    for i in (5, 6, 7):
        loads[i].wait()

    def owner_work(b):
        arrived(attb.at[b, pl.ds(0, N - 1)], recv_s.at[2 + b])

        def unpack(i):
            one, two = attb[b, 2 * i], attb[b, 2 * i + 1]
            attf[:, lanes(i, 128)] = jnp.concatenate([one[:, :HD], two[:, :HD]], axis=1)
            ef[:, lanes(i, 128)] = jnp.concatenate([one[:, HD:], two[:, HD:]], axis=1)

        loop(N // 2, unpack)
        seen = seencol[b, own64, :] > 0.0

        def update(i):
            cut = lanes(i, 256)
            inputs = jnp.where(seen, ef[:, cut].astype(F32), mask_r[:, cut]) + pos[own64, cut]
            updb[:, cut] = (inputs + nn(attf[...], wo[:, cut])).astype(BF16)

        loop(4, update)

        def predict(i):
            cut = lanes(i, 256)
            px = nn(updb[...], wp[:, cut])
            pred_o[b, :, cut] = px.astype(BF16)
            resid[:, cut] = jnp.where(seen, 0.0, px - tgt[b, :, cut].astype(F32)).astype(BF16)

        loop(3, predict)

        def grad_updated(i):
            gub[:, lanes(i, 256)] = nt(resid[...], wp[rows(i, 256), :]).astype(BF16)

        loop(4, grad_updated)

        def grad_attended(i):
            gab[:, lanes(i, 256)] = nt(gub[...], wo[rows(i, 256), :]).astype(BF16)

        loop(4, grad_attended)

        def pack(i):
            a, u = gab[:, lanes(i, 128)], gub[:, lanes(i, 128)]
            gsend[b, 2 * i] = jnp.concatenate([a[:, :HD], u[:, :HD]], axis=1)
            gsend[b, 2 * i + 1] = jnp.concatenate([a[:, HD:], u[:, HD:]], axis=1)

        loop(N // 2, pack)
        each_peer(lambda k: to(k, gsend.at[b, k], gall.at[b, own64], send_s.at[4 + b], recv_s.at[4 + b]).start())
        gall[b, own64, :] = gsend[b, m]

    loop(2, owner_work)

    def backward(b):
        arrived(gall.at[b, pl.ds(0, 960)], recv_s.at[4 + b])
        q, k, v = (qall[b, :, t * HD : (t + 1) * HD] for t in range(3))

        def keys_back(i, totals):
            r = rows(i, 256)
            wide = jnp.where(seencol[b, r, :] > 0.0, 0.0, gall[b, r, 0:HD].astype(F32))
            g = wide.astype(BF16)
            delta = jnp.sum(wide * attp[b, r, 0:HD].astype(F32), axis=1, keepdims=True)
            p = ps[b, r, :]
            ds = (p * (nt(g, qall[b, :, 2 * HD : 3 * HD]) - delta)).astype(BF16)
            return (totals[0] + tn(ds, qt[r, :]), totals[1] + tn(p.astype(BF16), g))

        nil = jnp.zeros((256, HD), F32)
        dk, dv = lax.fori_loop(0, 4, keys_back, (nil, nil))

        both = nn(take[b], gall[b])
        gv = both[:, 0:HD]
        delta = jnp.sum(gv * av[b].astype(F32), axis=1, keepdims=True)
        gv = gv.astype(BF16)
        p2 = p2s[b]
        ds1 = (p1s[b] * (nt(gv, vt[...]) - delta)).astype(BF16)
        ds2 = (p2 * (nt(gv, v) - delta)).astype(BF16)
        dq = (nn(ds1, kt[...]) + nn(ds2, k)) * 0.125
        dk = dk + tn(ds2, q)
        dv = dv + tn(p2.astype(BF16), gv)
        dpack[b, :, 0:HD] = dq.astype(BF16)
        dpack[b, :, HD : 2 * HD] = dk.astype(BF16)
        dpack[b, :, 2 * HD : 3 * HD] = dv.astype(BF16)
        dpack[b, :, 3 * HD :] = both[:, HD:].astype(BF16)
        each_peer(lambda k: to(k, dpack.at[b, rows(k, 16)], dbuf.at[b, m], send_s.at[6 + b], recv_s.at[6 + b]).start())
        dbuf[b, m] = dpack[b, mine, :]

    loop(2, backward)

    def norm_back(b):
        arrived(dbuf.at[b, pl.ds(0, N - 1)], recv_s.at[6 + b])

        def unpack(i):
            one, two = dbuf[b, 2 * i], dbuf[b, 2 * i + 1]
            for t in range(4):
                cut = slice(t * HD, (t + 1) * HD)
                df[t, :, lanes(i, 128)] = jnp.concatenate([one[:, cut], two[:, cut]], axis=1)

        loop(N // 2, unpack)

        def back_project(i):
            r = rows(i, 256)
            cut = lanes(i, 256)
            sc[:, cut] = (nt(df[0], wq[r, :]) + nt(df[1], wk[r, :]) + nt(df[2], wv[r, :])) * gain_r[:, cut]

        loop(4, back_project)
        scaled = sc[...]
        std = stdo[rows(b, 16), :]
        back = df[3].astype(F32) + invo[rows(b, 16), :] * (
            scaled
            - jnp.mean(scaled, axis=-1, keepdims=True)
            - std * jnp.mean(scaled * std, axis=-1, keepdims=True)
        )
        for q in range(PIECES):
            ret[q, b, mine, :] = back[:, q * WIDE : (q + 1) * WIDE].astype(BF16)
        for q in range(PIECES):
            block = ret.at[q, b, mine]
            each_peer(lambda k: to(k, block, block, ag2send.at[q, b], ag2_s.at[q, b]).start())

    loop(2, norm_back)

    def cross(src, dst, send, recv):
        return pltpu.make_async_remote_copy(
            src_ref=src, dst_ref=dst, send_sem=send, recv_sem=recv,
            device_id={"section": 1 - c}, device_id_type=MESH,
        )

    def z_copy(k, src, dst, send, recv):
        return pltpu.make_async_remote_copy(
            src_ref=src, dst_ref=dst, send_sem=send, recv_sem=recv,
            device_id={"dp": k}, device_id_type=MESH,
        )

    z_other = lax.rem(z + 1, NZ)
    firsts = [cross(loc.at[q, :, rows(1 - c, 192)], half_in.at[q], csend.at[q], crecv.at[q]) for q in range(PIECES)]
    for q in range(PIECES):
        for b in range(2):
            arrived(ret.at[q, b, pl.ds(0, 240)], ag2_s.at[q, b])

        def local_grad(t, q=q):
            both = nn(encT[...], ret[q, :, :, lanes(t, 256)].reshape(512, 256)).astype(BF16)
            loc[q, 2 * t] = both[:, :128]
            loc[q, 2 * t + 1] = both[:, 128:]

        loop(WIDE // 256, local_grad)
        firsts[q].start()

    for q in range(PIECES):
        firsts[q].wait_recv()

        def both_cores(d, q=q):
            t, deep = lax.rem(d, TILES), (d // TILES) * DEEP
            own_part = loc[q, t, pl.ds(pl.multiple_of(c * 192 + deep, DEEP), DEEP), :]
            their_part = half_in[q, t, pl.ds(pl.multiple_of(deep, DEEP), DEEP), :]
            zin[q, d] = (own_part.astype(F32) + their_part.astype(F32)).astype(BF16)

        loop(NZ, both_cores)
        each_z(lambda k, q=q: z_copy(k, zin.at[q, k], zbuf.at[q, z], zsend.at[q], z1_s.at[q]).start())

    forward = lambda q, k: cross(zgat.at[q, k], zown.at[q, k], fsend.at[q, k], frecv.at[q, k])
    for q in range(PIECES):
        z_copy(z_other, zbuf.at[q, pl.ds(0, NZ - 1)], zbuf.at[q, pl.ds(0, NZ - 1)], zsend.at[q], z1_s.at[q]).wait_recv()
        zbuf[q, z] = zin[q, z]
        total = zbuf[q, 0].astype(F32)
        for k in range(1, NZ):
            total = total + zbuf[q, k].astype(F32)
        zgat[q, z] = total.astype(BF16)
        each_z(lambda k, q=q: z_copy(k, zgat.at[q, z], zgat.at[q, z], z2send.at[q], z2_s.at[q, z]).start())
        forward(q, z).start()

    def encoder_grad(b):
        total = nt(ret[0, b], we[:, 0:WIDE])
        for q in range(1, PIECES):
            total = total + nt(ret[q, b], we[:, q * WIDE : (q + 1) * WIDE])
        encg_o[rows(b, 256), :] = total.astype(BF16)

    loop(2, encoder_grad)

    def get_z(q, k):
        z_copy(k, zgat.at[q, k], zgat.at[q, k], z2send.at[q], z2_s.at[q, k]).wait_recv()
        forward(q, k).start()

    def write(q, core, block):
        for d in range(NZ):
            at = pl.ds(pl.multiple_of(core * 192 + (d // TILES) * DEEP, DEEP), DEEP)
            col = q * WIDE + (d % TILES) * 128
            emb_o[at, col : col + 128] = block[q, d]

    for q in range(PIECES):
        each_z(lambda k, q=q: get_z(q, k))
        write(q, c, zgat)
    for q in range(PIECES):
        for k in range(NZ):
            forward(q, k).wait_recv()
        write(q, 1 - c, zown)

    left_here(rsbuf.at[pl.ds(0, N - 1)], send_s.at[0])
    left_here(qsend.at[pl.ds(0, N - 1)], send_s.at[1])
    for b in range(2):
        left_here(attb.at[b, pl.ds(0, N - 1)], send_s.at[2 + b])
        left_here(gsend.at[b, pl.ds(0, N - 1)], send_s.at[4 + b])
        left_here(dbuf.at[b, pl.ds(0, N - 1)], send_s.at[6 + b])
        for q in range(PIECES):
            left_here(ret.at[q, b, pl.ds(0, 240)], ag2send.at[q, b])
    for q in range(PIECES):
        firsts[q].wait_send()
        seven = zbuf.at[q, pl.ds(0, NZ - 1)]
        z_copy(z_other, seven, seven, zsend.at[q], z1_s.at[q]).wait_send()
        z_copy(z_other, seven, seven, z2send.at[q], z1_s.at[q]).wait_send()
        for k in range(NZ):
            forward(q, k).wait_send()


def finish(pred_i, encg_i, emb_i, pred_o, encg_o, emb_o):
    pred_o[...] = pred_i[...]
    encg_o[...] = encg_i[...]
    emb_o[...] = emb_i[...].astype(F32) * 8192 ** (-0.5)


def body(
    encoded, visible, owner, embed_weight, mask_token, norm_gain,
    query_weight, key_weight, value_weight, out_weight, pixel_weight, targets,
):
    quarter = 256
    freqs = 10000.0 ** (-jnp.arange(quarter, dtype=F32) / quarter)
    angle = jnp.arange(GRID, dtype=F32)[:, None] * freqs[None, :]
    trig = jnp.concatenate([jnp.sin(angle), jnp.cos(angle)], axis=1)
    vm = pl.BlockSpec(memory_space=pltpu.VMEM)
    hbm = pl.BlockSpec(memory_space=pl.ANY)
    V = pltpu.VMEM
    dma = pltpu.SemaphoreType.DMA
    scratch = [
        V((512, 384), BF16), V((384, 1024), BF16),
        V((1024, 1024), BF16), V((1024, 1024), BF16), V((1024, 1024), BF16), V((1024, 1024), BF16),
        V((1024, 768), BF16), V((2, 64, 768), BF16),
        V((2, 256, 1024), BF16), V((N, 2, 16, 1024), BF16), V((384, 512), BF16),
        V((1024, 1), F32), V((2, 256, 1), F32), V((2, 1, 1024), F32), V((2, 1024, 1), F32),
        V((2, 1024, 256), BF16), V((2, 256, 1024), BF16), V((192, 1024), BF16),
        V((1024, 1024), F32), V((32, 1024), F32), V((32, 1024), F32), V((32, 1), F32), V((1024, 192), BF16),
        V((1024, HD), BF16), V((1024, HD), BF16), V((1024, HD), BF16),
        V((2, 1024, 1), F32), V((2, 1024, 1), F32), V((2, 1024, HD), F32),
        V((32, 1024), BF16), V((4, 32, 1024), BF16), V((N, 2, 16, 256), BF16), V((2, 256, 256), BF16), V((2, 256, HD), BF16), V((2, 256, 2 * HD), BF16),
        V((2, 256, 1024), F32), V((2, 256, 256), F32), V((2, 1024, 256), F32),
        V((2, 1024, 128), BF16), V((2, N, 64, 128), BF16), V((64, 1024), BF16), V((64, 1024), BF16),
        V((64, 1024), BF16), V((64, 768), BF16), V((64, 1024), BF16), V((64, 1024), BF16),
        V((2, N, 64, 128), BF16), V((2, 1024, 128), BF16), V((2, 256, 256), BF16), V((2, N, 16, 256), BF16),
        V((4, 16, 1024), BF16), V((16, 1024), F32), V((PIECES, 2, 256, WIDE), BF16),
        V((PIECES, TILES, 384, 128), BF16), V((PIECES, TILES, 192, 128), BF16),
        V((PIECES, NZ, DEEP, 128), BF16), V((PIECES, NZ, DEEP, 128), BF16),
        V((PIECES, NZ, DEEP, 128), BF16), V((PIECES, NZ, DEEP, 128), BF16),
        dma((8,)), dma((8,)), dma((8,)), dma((PIECES, 2)), dma((PIECES, 2)),
        dma((PIECES,)), dma((PIECES,)), dma((PIECES,)), dma((PIECES, NZ)),
        dma((PIECES,)), dma((PIECES,)), dma((PIECES, NZ)), dma((PIECES, NZ)),
    ]
    predicted, encoded_grad, summed = pl.pallas_call(
        kernel,
        out_shape=(
            jax.ShapeDtypeStruct((2, 64, 768), BF16),
            jax.ShapeDtypeStruct((512, 384), BF16),
            jax.ShapeDtypeStruct((384, 1024), BF16),
        ),
        in_specs=[hbm, hbm, vm, vm, vm, vm, hbm, hbm, hbm, hbm, hbm, hbm, vm],
        out_specs=(vm, vm, vm),
        scratch_shapes=scratch,
        compiler_params=pltpu.CompilerParams(
            collective_id=0, has_side_effects=True, vmem_limit_bytes=58 * 1024 * 1024
        ),
        cost_estimate=pl.CostEstimate(flops=8_000_000_000, bytes_accessed=16_000_000, transcendentals=4_000_000),
    )(
        encoded, embed_weight, owner.reshape(1, 1024), visible.reshape(2, 1, 256), mask_token.reshape(1, 1024), norm_gain.reshape(1, 1024),
        query_weight, key_weight, value_weight, out_weight, pixel_weight, targets, trig,
    )
    return pl.pallas_call(
        finish,
        out_shape=(
            jax.ShapeDtypeStruct((2, 64, 768), BF16),
            jax.ShapeDtypeStruct((512, 384), BF16),
            jax.ShapeDtypeStruct((384, 1024), F32),
        ),
        in_specs=[vm, vm, vm],
        out_specs=(vm, vm, vm),
        cost_estimate=pl.CostEstimate(flops=400_000, bytes_accessed=3_500_000, transcendentals=0),
    )(predicted, encoded_grad, summed)


def solution(mesh):
    placed = (
        P(("dp", "section"), "mp"),
        P(("dp", "section"), None),
        P(),
        P("mp", None),
        P(),
        P(),
        P(),
        P(),
        P(),
        P(),
        P(),
        P(("dp", "section"), "mp", None),
    )
    return jax.shard_map(
        body,
        mesh=mesh,
        in_specs=placed,
        out_specs=(P(("dp", "section"), "mp", None), P(("dp", "section"), "mp"), P("mp", None)),
        check_vma=False,
    )
```

time: 125 us -> 111 us (0.89)
  Pallas kernels: 118 us -> 109 us
  local copies, waits for them, and re-layouts: 6.12 us -> 1.26 us
    pallas_call x1, Pallas kernels: 118 us -> 106 us  [body(): pl.pallas_call(kernel, out_shape=(jax.ShapeDtypeStruct((2, 64, 768), BF16...]
    unnamed x3 -> x0, local copies, waits for them, and re-layouts: 6.12 us -> none
    pallas_call x0 -> x1, Pallas kernels: none -> 2.72 us  [body(): pl.pallas_call(finish, out_shape=(jax.ShapeDtypeStruct((2, 64, 768), BF16...]
    reshape x0 -> x1, local copies, waits for them, and re-layouts: none -> 1.26 us  [body(): visible.reshape(2, 1, 256)]
where the time goes in v3:
time: 111 us
  Pallas kernels  109 us (98%)
  local copies, waits for them, and re-layouts  1.26 us (1%)
    pallas_call x1, Pallas kernels, body(): pl.pallas_call(kernel, out_shape=(jax.ShapeDtypeStruct((2, 64, 768), BF16...  106 us
    pallas_call x1, Pallas kernels, body(): pl.pallas_call(finish, out_shape=(jax.ShapeDtypeStruct((2, 64, 768), BF16...  2.72 us

profile of v3, /device:TPU:1, one launch (start us, length us, event | category | flops | bytes accessed | tf_op | source)
XLA Modules:
  0.0 111.2 jit_solution(185203327596821870)
XLA Ops:
  0.6 1.3 %reshape.25.vis_r = s32[2,1,256]{2,1,0:T(1,128)} reshape(s32[2,256]{1,0:T(2,128)} %param.13) | data formatting | bytes 4096 | tf_op jit(solution)/shard_map/reshape | solution.py:567
  1.9 0.1 fusion.1
  2.0 0.6 pad_maximum_fusion.trig_r
  2.7 105.8 %shard_map.139 = (bf16[2,64,768]{2,1,0:T(8,128)(2,1)}, bf16[512,384]{1,0:T(8,128)(2,1)}, bf16[384,1024]{1,0:T(8,128)(2,1)}) custom-call(bf16[512,384]{1,0:T(8,128)(2,1)} %enc_h.1, bf16[384,1024]{1,0:T(8,128)(2,1)} %we_h.1, s32[1,1024]{1,0:T(1,128)} %bitcast.3, s32[2,1,256]{2,1,0:T(1,128)} %reshape.25.vis_r, f32[1,1024]{1,0:T(1,128)} %bitcast.4, ...), custom_call_target="tpu_custom_call" | custom-call | flops 8000000000 | bytes 16000000 | tf_op jit(solution)/shard_map/pallas_call | solution.py:552
  108.5 2.7 %shard_map.140 = (bf16[2,64,768]{2,1,0:T(8,128)(2,1)}, bf16[512,384]{1,0:T(8,128)(2,1)}, f32[384,1024]{1,0:T(8,128)}) custom-call(bf16[2,64,768]{2,1,0:T(8,128)(2,1)} %get-tuple-element.6.pred_i, bf16[512,384]{1,0:T(8,128)(2,1)} %get-tuple-element.7.encg_i, bf16[384,1024]{1,0:T(8,128)(2,1)} %get-tuple-element.8.emb_i), custom_call_target="tpu_custom_call" | custom-call | flops 400000 | bytes 3500000 | tf_op jit(solution)/shard_map/pallas_call | solution.py:570
  (1 shorter events, 0.0 us)

commit v4 on v3

--- a/solution.py
+++ b/solution.py
@@ -14,6 +14,7 @@
 N = 16
 NZ = 8
 HD = 64
+OWN = 64
 PIECES = 2
 WIDE = 1024 // PIECES
 TILES = WIDE // 128
@@ -47,7 +48,14 @@
 
 
 def lanes(i, size):
+    if isinstance(i, int):
+        return slice(i * size, (i + 1) * size)
     return pl.ds(pl.multiple_of(i * size, size), size)
+
+
+def unrolled(n, f):
+    for i in range(n):
+        f(i)
 
 
 def loop(n, f):
@@ -58,8 +66,7 @@
     lax.fori_loop(0, n, one, 0)
 
 
-def rows(i, size):
-    return pl.ds(pl.multiple_of(i * size, size), size)
+rows = lanes
 
 
 def kernel(
@@ -67,7 +74,7 @@
     pred_o, encg_o, emb_o,
     enc, we, wq, wk, wv, wo, wp, tgt,
     part, rsbuf, encT,
-    placec, viscol, seenrow, seencol, put, take, ptab, pos, xown, stdo, invo, wh,
+    order, seenrow, seencol, put, take, ptab, pos, xown, stdo, invo, wh,
     qt, kt, vt, mt, lt, acc,
     normed, fs, qsend, qall, av, ave, p1s, p2s, ps,
     attp, attb, attf, ef, updb, resid, gub, gab, gsend, gall, dpack, dbuf, df, sc, ret,
@@ -134,49 +141,78 @@
     pl.semaphore_wait(barrier, N - 1 + NZ - 1 + 1)
     each_peer(lambda k: to(k, part.at[:, rows(k, 16)], rsbuf.at[m], send_s.at[0], recv_s.at[0]).start())
 
-    key_row = own_r[...].astype(F32) * 1024.0 + fiota((1, 1024), 1)
-    lane = fiota((256, 1024), 1)
-
-    def places(i, place_row):
-        s = fiota((256, 1024), 0) + (i * 256).astype(F32)
-        key_col = jnp.sum(jnp.where(lane == s, key_row, 0.0), axis=1, keepdims=True)
-        less = jnp.where(key_row < key_col, 1.0, 0.0)
-        placec[rows(i, 256), :] = jnp.sum(less, axis=1, keepdims=True)
-        more = jnp.where(key_col < key_row, 1.0, 0.0)
-        return place_row + jnp.sum(more, axis=0, keepdims=True)
-
-    place_row = lax.fori_loop(0, 4, places, jnp.zeros((1, 1024), F32))
-
-    def visible_places(b):
-        vrow = vis_r[b].astype(F32)
-        vcol = jnp.sum(jnp.where(fiota((256, 256), 0) == fiota((256, 256), 1), vrow, 0.0), axis=1, keepdims=True)
-        viscol[b] = vcol
-        vpc = jnp.sum(jnp.where(lane == vcol, place_row, 0.0), axis=1, keepdims=True)
-        vpr = jnp.sum(jnp.where(fiota((1024, 256), 0) == vrow, placec[...], 0.0), axis=0, keepdims=True)
-        gather = jnp.where(vpc == lane, 1.0, 0.0)
-        seenrow[b] = jnp.sum(gather, axis=0, keepdims=True)
-        take[b] = gather.astype(BF16)
-        spread = jnp.where(vpr == fiota((1024, 256), 0), 1.0, 0.0)
-        seencol[b] = jnp.sum(spread, axis=1, keepdims=True)
-        put[b] = spread.astype(BF16)
-
-    loop(2, visible_places)
+    owner_row = own_r[...].astype(F32)
+    of_owner = jnp.where(owner_row == fiota((N, 1024), 0), 1.0, 0.0)
+    before = hot(fiota((128, 128), 0) < fiota((128, 128), 1))
+    carry = jnp.zeros((N, 1), F32)
+    ranks = []
+    for a in range(8):
+        block = of_owner[:, a * 128 : (a + 1) * 128]
+        prior = nn(block.astype(BF16), before) + carry
+        carry = carry + jnp.sum(block, axis=1, keepdims=True)
+        ranks.append(jnp.sum(prior * block, axis=0, keepdims=True))
+    rank_row = jnp.concatenate(ranks, axis=1)
+    patch_ids = lax.broadcasted_iota(jnp.int32, (N, 1024), 1)
+    halves = jnp.concatenate(
+        [of_owner * (patch_ids >> 5).astype(F32), of_owner * (patch_ids & 31).astype(F32)], axis=0
+    ).astype(BF16)
+    order[...] = nt(hot(rank_row == fiota((OWN, 1024), 0)), halves)
+
+    def order_col(o):
+        return jnp.sum(jnp.where(fiota((OWN, 2 * N), 1) == o, order[...], 0.0), axis=1, keepdims=True)
+
+    lookup = jnp.concatenate(
+        [owner_row[:, a * 128 : (a + 1) * 128] for a in range(8)] + [ranks[a] for a in range(8)], axis=0
+    ).astype(BF16)
+    eye = fiota((256, 256), 0) == fiota((256, 256), 1)
+    lane = lax.broadcasted_iota(jnp.int32, (256, 128), 1)
+    own_patch = []
+    for b in range(2):
+        vrow = vis_r[b : b + 1, :]
+        found = nn(lookup, hot(lax.broadcasted_iota(jnp.int32, (128, 256), 0) == (vrow & 127)))
+        part_of = lax.broadcasted_iota(jnp.int32, (8, 256), 0) == (vrow >> 7)
+        vis_owner = jnp.sum(jnp.where(part_of, found[0:8], 0.0), axis=0, keepdims=True)
+        vis_rank = jnp.sum(jnp.where(part_of, found[8:16], 0.0), axis=0, keepdims=True)
+        by_rank = hot(vis_rank == fiota((OWN, 256), 0))
+        for o in range(N):
+            put[b, o * OWN : (o + 1) * OWN, :] = by_rank * hot(vis_owner == float(o))
+        owner_col = jnp.sum(jnp.where(eye, vis_owner, 0.0), axis=1, keepdims=True)
+        rank_col = jnp.sum(jnp.where(eye, vis_rank, 0.0), axis=1, keepdims=True)
+        by_rank = hot(rank_col == (lane & 63).astype(F32))
+        owner_lane = (lane >> 6).astype(F32)
+        for t in range(8):
+            take[b, :, t * 128 : (t + 1) * 128] = by_rank * hot(owner_col - 2.0 * t == owner_lane)
+        seenrow[b] = nn(jnp.ones((N, 256), BF16), take[b])[0:1]
+        seencol[b] = nn(put[b], jnp.ones((256, 128), BF16))[:, 0:1]
+        mine_at = fiota((16, 256), 1) == fiota((16, 256), 0) + (m * 16).astype(F32)
+        own_patch.append(jnp.sum(jnp.where(mine_at, vrow.astype(F32), 0.0), axis=1, keepdims=True))
 
     trig = trig_r[...]
     hi = trig.astype(BF16)
     rest = trig - hi.astype(F32)
     mid = rest.astype(BF16)
     low = (rest - mid.astype(F32)).astype(BF16)
+    token = mask_r[...]
+    token_hi = token.astype(BF16)
+    rest = token - token_hi.astype(F32)
+    token_mid = rest.astype(BF16)
+    token_low = (rest - token_mid.astype(F32)).astype(BF16)
     ptab[...] = jnp.zeros_like(ptab)
     for i, term in enumerate((hi, mid, low)):
         ptab[32 * i : 32 * i + 32, 0:512] = term
         ptab[96 + 32 * i : 128 + 32 * i, 512:1024] = term
-
-    def positions(patch_col):
-        patch = patch_col.astype(jnp.int32)
-        which = lax.broadcasted_iota(jnp.int32, (patch.shape[0], 192), 1)
-        want = jnp.where(which < 96, patch >> 5, patch & 31)
-        return nn(hot((which & 31) == want), ptab[...])
+    for i, term in enumerate((token_hi, token_mid, token_low)):
+        ptab[192 + 16 * i : 208 + 16 * i, :] = jnp.where(
+            lax.broadcasted_iota(jnp.int32, (16, 1024), 0) == 0, term.astype(F32), 0.0
+        ).astype(BF16)
+
+    def positions(row, col, with_token):
+        which = lax.broadcasted_iota(jnp.int32, (row.shape[0], 256), 1)
+        want = jnp.where(which < 96, row, col)
+        picked = (which & 31).astype(F32) == want
+        last = (which & 15 == 0) if with_token else (which < 0)
+        one = jnp.where(which < 192, jnp.where(picked, 1.0, 0.0), jnp.where(last, 1.0, 0.0))
+        return nn(one.astype(BF16), ptab[...])
 
     for i in (2, 3, 4):
         loads[i].wait()
@@ -187,23 +223,36 @@
         wh[:, i * HD : (i + 1) * HD] = jnp.where(odd, two[:, HD:], two[:, :HD]).astype(BF16)
 
     gain = gain_r[...]
-    token = mask_r[...]
     scale = jnp.array(0.125, BF16)
 
     def masked(i):
         r = rows(i, 256)
-        s = fiota((256, 1024), 0) + (i * 256).astype(F32)
-        order = jnp.sum(jnp.where(place_row == s, lane, 0.0), axis=1, keepdims=True)
-        p = positions(order)
-        pos[r, :] = p
-        std, _ = norm(token + p)
+        owners = [(4 * i + j).astype(F32) for j in range(4)]
+        row = jnp.concatenate([order_col(o) for o in owners], axis=0)
+        col = jnp.concatenate([order_col(o + N) for o in owners], axis=0)
+        std, _ = norm(positions(row, col, True))
         three = nn((std * gain).astype(BF16), wh[...]).astype(BF16)
         qt[r, :] = three[:, 0:HD] * scale
         kt[r, :] = three[:, HD : 2 * HD]
         vt[r, :] = three[:, 2 * HD :]
 
     loop(4, masked)
-    xown[...] = positions(jnp.concatenate([viscol[0, mine, :], viscol[1, mine, :]], axis=0))
+    def table(i):
+        r = rows(i, 256)
+        s = nt(qt[r, :], kt[...])
+        for b in range(2):
+            held = jnp.where(seenrow[b] > 0.0, -jnp.inf, s)
+            top = jnp.max(held, axis=1, keepdims=True)
+            e = jnp.exp(held - top)
+            mt[b, r, :] = top
+            lt[b, r, :] = jnp.sum(e, axis=1, keepdims=True)
+            acc[b, r, :] = nn(e.astype(BF16), vt[...])
+
+    loop(2, table)
+    ids = jnp.concatenate(own_patch, axis=0).astype(jnp.int32)
+    xown[...] = positions((ids >> 5).astype(F32), (ids & 31).astype(F32), False)
+    own_position = positions(order_col(m.astype(F32)), order_col((m + N).astype(F32)), False)
+    pos[...] = own_position
 
     arrived(rsbuf.at[pl.ds(0, N - 1)], recv_s.at[0])
     rsbuf[m] = part[:, mine, :]
@@ -222,7 +271,7 @@
         fs[1, :, cut] = nn(normed[...], wk[:, cut]).astype(BF16)
         fs[2, :, cut] = nn(normed[...], wv[:, cut]).astype(BF16)
 
-    loop(4, project)
+    unrolled(4, project)
 
     def pack_rows(i):
         for t in range(4):
@@ -230,22 +279,11 @@
             qsend[2 * i, :, :, t * HD : (t + 1) * HD] = two[:, :, :HD]
             qsend[2 * i + 1, :, :, t * HD : (t + 1) * HD] = two[:, :, HD:]
 
-    loop(N // 2, pack_rows)
+    unrolled(N // 2, pack_rows)
     each_peer(lambda k: to(k, qsend.at[k], qall.at[:, mine], send_s.at[1], recv_s.at[1]).start())
     qall[:, mine, :] = qsend[m]
 
-    def table(i):
-        r = rows(i, 256)
-        s = nt(qt[r, :], kt[...])
-        for b in range(2):
-            held = jnp.where(seenrow[b] > 0.0, -jnp.inf, s)
-            top = jnp.max(held, axis=1, keepdims=True)
-            e = jnp.exp(held - top)
-            mt[b, r, :] = top
-            lt[b, r, :] = jnp.sum(e, axis=1, keepdims=True)
-            acc[b, r, :] = nn(e.astype(BF16), vt[...])
-
-    loop(4, table)
+    lax.fori_loop(2, 4, lambda i, _: (table(i), 0)[1], 0)
     encT[...] = jnp.transpose(enc[...])
 
     arrived(qall.at[:, pl.ds(0, 240)], recv_s.at[1])
@@ -297,7 +335,7 @@
         lax.fori_loop(1, 5, attend, 0)
         attb[b, m] = attp[b, own64, :]
 
-    loop(2, attention)
+    unrolled(2, attention)
 
     for i in (5, 6, 7):
         loads[i].wait()
@@ -310,15 +348,15 @@
             attf[:, lanes(i, 128)] = jnp.concatenate([one[:, :HD], two[:, :HD]], axis=1)
             ef[:, lanes(i, 128)] = jnp.concatenate([one[:, HD:], two[:, HD:]], axis=1)
 
-        loop(N // 2, unpack)
+        unrolled(N // 2, unpack)
         seen = seencol[b, own64, :] > 0.0
 
         def update(i):
             cut = lanes(i, 256)
-            inputs = jnp.where(seen, ef[:, cut].astype(F32), mask_r[:, cut]) + pos[own64, cut]
+            inputs = jnp.where(seen, ef[:, cut].astype(F32), mask_r[:, cut]) + pos[:, cut]
             updb[:, cut] = (inputs + nn(attf[...], wo[:, cut])).astype(BF16)
 
-        loop(4, update)
+        unrolled(4, update)
 
         def predict(i):
             cut = lanes(i, 256)
@@ -326,28 +364,28 @@
             pred_o[b, :, cut] = px.astype(BF16)
             resid[:, cut] = jnp.where(seen, 0.0, px - tgt[b, :, cut].astype(F32)).astype(BF16)
 
-        loop(3, predict)
+        unrolled(3, predict)
 
         def grad_updated(i):
             gub[:, lanes(i, 256)] = nt(resid[...], wp[rows(i, 256), :]).astype(BF16)
 
-        loop(4, grad_updated)
+        unrolled(4, grad_updated)
 
         def grad_attended(i):
             gab[:, lanes(i, 256)] = nt(gub[...], wo[rows(i, 256), :]).astype(BF16)
 
-        loop(4, grad_attended)
+        unrolled(4, grad_attended)
 
         def pack(i):
             a, u = gab[:, lanes(i, 128)], gub[:, lanes(i, 128)]
             gsend[b, 2 * i] = jnp.concatenate([a[:, :HD], u[:, :HD]], axis=1)
             gsend[b, 2 * i + 1] = jnp.concatenate([a[:, HD:], u[:, HD:]], axis=1)
 
-        loop(N // 2, pack)
+        unrolled(N // 2, pack)
         each_peer(lambda k: to(k, gsend.at[b, k], gall.at[b, own64], send_s.at[4 + b], recv_s.at[4 + b]).start())
         gall[b, own64, :] = gsend[b, m]
 
-    loop(2, owner_work)
+    unrolled(2, owner_work)
 
     def backward(b):
         arrived(gall.at[b, pl.ds(0, 960)], recv_s.at[4 + b])
@@ -382,7 +420,7 @@
         each_peer(lambda k: to(k, dpack.at[b, rows(k, 16)], dbuf.at[b, m], send_s.at[6 + b], recv_s.at[6 + b]).start())
         dbuf[b, m] = dpack[b, mine, :]
 
-    loop(2, backward)
+    unrolled(2, backward)
 
     def norm_back(b):
         arrived(dbuf.at[b, pl.ds(0, N - 1)], recv_s.at[6 + b])
@@ -393,14 +431,14 @@
                 cut = slice(t * HD, (t + 1) * HD)
                 df[t, :, lanes(i, 128)] = jnp.concatenate([one[:, cut], two[:, cut]], axis=1)
 
-        loop(N // 2, unpack)
+        unrolled(N // 2, unpack)
 
         def back_project(i):
             r = rows(i, 256)
             cut = lanes(i, 256)
             sc[:, cut] = (nt(df[0], wq[r, :]) + nt(df[1], wk[r, :]) + nt(df[2], wv[r, :])) * gain_r[:, cut]
 
-        loop(4, back_project)
+        unrolled(4, back_project)
         scaled = sc[...]
         std = stdo[rows(b, 16), :]
         back = df[3].astype(F32) + invo[rows(b, 16), :] * (
@@ -414,7 +452,7 @@
             block = ret.at[q, b, mine]
             each_peer(lambda k: to(k, block, block, ag2send.at[q, b], ag2_s.at[q, b]).start())
 
-    loop(2, norm_back)
+    unrolled(2, norm_back)
 
     def cross(src, dst, send, recv):
         return pltpu.make_async_remote_copy(
@@ -439,19 +477,19 @@
             loc[q, 2 * t] = both[:, :128]
             loc[q, 2 * t + 1] = both[:, 128:]
 
-        loop(WIDE // 256, local_grad)
+        unrolled(WIDE // 256, local_grad)
         firsts[q].start()
 
     for q in range(PIECES):
         firsts[q].wait_recv()
 
         def both_cores(d, q=q):
-            t, deep = lax.rem(d, TILES), (d // TILES) * DEEP
+            t, deep = d % TILES, (d // TILES) * DEEP
             own_part = loc[q, t, pl.ds(pl.multiple_of(c * 192 + deep, DEEP), DEEP), :]
-            their_part = half_in[q, t, pl.ds(pl.multiple_of(deep, DEEP), DEEP), :]
+            their_part = half_in[q, t, deep : deep + DEEP, :]
             zin[q, d] = (own_part.astype(F32) + their_part.astype(F32)).astype(BF16)
 
-        loop(NZ, both_cores)
+        unrolled(NZ, both_cores)
         each_z(lambda k, q=q: z_copy(k, zin.at[q, k], zbuf.at[q, z], zsend.at[q], z1_s.at[q]).start())
 
     forward = lambda q, k: cross(zgat.at[q, k], zown.at[q, k], fsend.at[q, k], frecv.at[q, k])
@@ -471,7 +509,7 @@
             total = total + nt(ret[q, b], we[:, q * WIDE : (q + 1) * WIDE])
         encg_o[rows(b, 256), :] = total.astype(BF16)
 
-    loop(2, encoder_grad)
+    unrolled(2, encoder_grad)
 
     def get_z(q, k):
         z_copy(k, zgat.at[q, k], zgat.at[q, k], z2send.at[q], z2_s.at[q, k]).wait_recv()
@@ -531,9 +569,9 @@
         V((1024, 1024), BF16), V((1024, 1024), BF16), V((1024, 1024), BF16), V((1024, 1024), BF16),
         V((1024, 768), BF16), V((2, 64, 768), BF16),
         V((2, 256, 1024), BF16), V((N, 2, 16, 1024), BF16), V((384, 512), BF16),
-        V((1024, 1), F32), V((2, 256, 1), F32), V((2, 1, 1024), F32), V((2, 1024, 1), F32),
-        V((2, 1024, 256), BF16), V((2, 256, 1024), BF16), V((192, 1024), BF16),
-        V((1024, 1024), F32), V((32, 1024), F32), V((32, 1024), F32), V((32, 1), F32), V((1024, 192), BF16),
+        V((OWN, 2 * N), F32), V((2, 1, 1024), F32), V((2, 1024, 1), F32),
+        V((2, 1024, 256), BF16), V((2, 256, 1024), BF16), V((256, 1024), BF16),
+        V((OWN, 1024), F32), V((32, 1024), F32), V((32, 1024), F32), V((32, 1), F32), V((1024, 192), BF16),
         V((1024, HD), BF16), V((1024, HD), BF16), V((1024, HD), BF16),
         V((2, 1024, 1), F32), V((2, 1024, 1), F32), V((2, 1024, HD), F32),
         V((32, 1024), BF16), V((4, 32, 1024), BF16), V((N, 2, 16, 256), BF16), V((2, 256, 256), BF16), V((2, 256, HD), BF16), V((2, 256, 2 * HD), BF16),
@@ -564,7 +602,7 @@
         ),
         cost_estimate=pl.CostEstimate(flops=8_000_000_000, bytes_accessed=16_000_000, transcendentals=4_000_000),
     )(
-        encoded, embed_weight, owner.reshape(1, 1024), visible.reshape(2, 1, 256), mask_token.reshape(1, 1024), norm_gain.reshape(1, 1024),
+        encoded, embed_weight, owner.reshape(1, 1024), visible, mask_token.reshape(1, 1024), norm_gain.reshape(1, 1024),
         query_weight, key_weight, value_weight, out_weight, pixel_weight, targets, trig,
     )
     return pl.pallas_call(

time: 111 us -> 104 us (0.937)
  Pallas kernels: 109 us -> 103 us
  local copies, waits for them, and re-layouts: 1.26 us -> 0 us
    pallas_call x1, Pallas kernels: 106 us -> 99.9 us  [body(): pl.pallas_call(kernel, out_shape=(jax.ShapeDtypeStruct((2, 64, 768), BF16...]
    reshape x1 -> x0, local copies, waits for them, and re-layouts: 1.26 us -> none  [body(): visible.reshape(2, 1, 256)]
where the time goes in v4:
time: 104 us
  Pallas kernels  103 us (99%)
    pallas_call x1, Pallas kernels, body(): pl.pallas_call(kernel, out_shape=(jax.ShapeDtypeStruct((2, 64, 768), BF16...  99.9 us
    pallas_call x1, Pallas kernels, body(): pl.pallas_call(finish, out_shape=(jax.ShapeDtypeStruct((2, 64, 768), BF16...  2.72 us

profile of v4, /device:TPU:1, one launch (start us, length us, event | category | flops | bytes accessed | tf_op | source)
XLA Modules:
  0.0 104.1 jit_solution(8624742470489949666)
XLA Ops:
  0.6 0.1 fusion.1
  0.8 0.6 pad_maximum_fusion.trig_r
  1.4 99.9 %shard_map.139 = (bf16[2,64,768]{2,1,0:T(8,128)(2,1)}, bf16[512,384]{1,0:T(8,128)(2,1)}, bf16[384,1024]{1,0:T(8,128)(2,1)}) custom-call(bf16[512,384]{1,0:T(8,128)(2,1)} %enc_h.1, bf16[384,1024]{1,0:T(8,128)(2,1)} %we_h.1, s32[1,1024]{1,0:T(1,128)} %bitcast.3, s32[2,256]{1,0:T(2,128)} %vis_r.1, f32[1,1024]{1,0:T(1,128)} %bitcast.4, f32[1,1024]{1,0:T(1,128)} %bitcast.5, ...), custom_call_target="tpu_custom_call" | custom-call | flops 8000000000 | bytes 16000000 | tf_op jit(solution)/shard_map/pallas_call | solution.py:590
  101.4 2.7 %shard_map.140 = (bf16[2,64,768]{2,1,0:T(8,128)(2,1)}, bf16[512,384]{1,0:T(8,128)(2,1)}, f32[384,1024]{1,0:T(8,128)}) custom-call(bf16[2,64,768]{2,1,0:T(8,128)(2,1)} %get-tuple-element.6.pred_i, bf16[512,384]{1,0:T(8,128)(2,1)} %get-tuple-element.7.encg_i, bf16[384,1024]{1,0:T(8,128)(2,1)} %get-tuple-element.8.emb_i), custom_call_target="tpu_custom_call" | custom-call | flops 400000 | bytes 3500000 | tf_op jit(solution)/shard_map/pallas_call | solution.py:608
  (1 shorter events, 0.0 us)

commit v5 on v4

--- a/solution.py
+++ b/solution.py
@@ -74,7 +74,7 @@
     pred_o, encg_o, emb_o,
     enc, we, wq, wk, wv, wo, wp, tgt,
     part, rsbuf, encT,
-    order, seenrow, seencol, put, take, ptab, pos, xown, stdo, invo, wh,
+    order, seenrow, seencol, put, take, ptab, ttab, pos, xown, stdo, invo, wh,
     qt, kt, vt, mt, lt, acc,
     normed, fs, qsend, qall, av, ave, p1s, p2s, ps,
     attp, attb, attf, ef, updb, resid, gub, gab, gsend, gall, dpack, dbuf, df, sc, ret,
@@ -137,9 +137,24 @@
         part[0, rows(g, 64), :] = out[:64]
         part[1, rows(g, 64), :] = out[64:]
 
-    loop(4, partial_block)
+    my_group = m // 4
+
+    def send_part(k):
+        to(k, part.at[:, rows(k, 16)], rsbuf.at[m], send_s.at[0], recv_s.at[0]).start()
+
+    partial_block(lax.rem(my_group + 1, 4))
     pl.semaphore_wait(barrier, N - 1 + NZ - 1 + 1)
-    each_peer(lambda k: to(k, part.at[:, rows(k, 16)], rsbuf.at[m], send_s.at[0], recv_s.at[0]).start())
+
+    def send_group(jj, _):
+        g = lax.rem(my_group + jj, 4)
+        for i in range(4):
+            send_part(4 * g + i)
+        partial_block(lax.rem(g + 1, 4))
+        return 0
+
+    lax.fori_loop(1, 4, send_group, 0)
+    for i in range(1, 4):
+        send_part(4 * my_group + lax.rem(m + i, 4))
 
     owner_row = own_r[...].astype(F32)
     of_owner = jnp.where(owner_row == fiota((N, 1024), 0), 1.0, 0.0)
@@ -187,32 +202,24 @@
         mine_at = fiota((16, 256), 1) == fiota((16, 256), 0) + (m * 16).astype(F32)
         own_patch.append(jnp.sum(jnp.where(mine_at, vrow.astype(F32), 0.0), axis=1, keepdims=True))
 
+    def terms(x):
+        hi = x.astype(BF16)
+        rest = x - hi.astype(F32)
+        mid = rest.astype(BF16)
+        return hi, mid, (rest - mid.astype(F32)).astype(BF16)
+
     trig = trig_r[...]
-    hi = trig.astype(BF16)
-    rest = trig - hi.astype(F32)
-    mid = rest.astype(BF16)
-    low = (rest - mid.astype(F32)).astype(BF16)
-    token = mask_r[...]
-    token_hi = token.astype(BF16)
-    rest = token - token_hi.astype(F32)
-    token_mid = rest.astype(BF16)
-    token_low = (rest - token_mid.astype(F32)).astype(BF16)
     ptab[...] = jnp.zeros_like(ptab)
-    for i, term in enumerate((hi, mid, low)):
+    for i, term in enumerate(terms(trig)):
         ptab[32 * i : 32 * i + 32, 0:512] = term
         ptab[96 + 32 * i : 128 + 32 * i, 512:1024] = term
-    for i, term in enumerate((token_hi, token_mid, token_low)):
-        ptab[192 + 16 * i : 208 + 16 * i, :] = jnp.where(
-            lax.broadcasted_iota(jnp.int32, (16, 1024), 0) == 0, term.astype(F32), 0.0
-        ).astype(BF16)
-
-    def positions(row, col, with_token):
-        which = lax.broadcasted_iota(jnp.int32, (row.shape[0], 256), 1)
-        want = jnp.where(which < 96, row, col)
-        picked = (which & 31).astype(F32) == want
-        last = (which & 15 == 0) if with_token else (which < 0)
-        one = jnp.where(which < 192, jnp.where(picked, 1.0, 0.0), jnp.where(last, 1.0, 0.0))
-        return nn(one.astype(BF16), ptab[...])
+
+    def row_and_col(row, col):
+        which = lax.broadcasted_iota(jnp.int32, (row.shape[0], 192), 1)
+        return hot((which & 31).astype(F32) == jnp.where(which < 96, row, col))
+
+    def positions(row, col):
+        return nn(row_and_col(row, col), ptab[...])
 
     for i in (2, 3, 4):
         loads[i].wait()
@@ -225,13 +232,35 @@
     gain = gain_r[...]
     scale = jnp.array(0.125, BF16)
 
+    def gained(x, gains, w):
+        out = nn(jnp.concatenate(terms(x * gains), axis=0), w)
+        n = x.shape[0]
+        return out[0:n] + out[n : 2 * n] + out[2 * n : 3 * n]
+
+    ones_gain = gained(jnp.ones((16, 1024), F32), gain, wh[...])[0:1]
+    at_lane = lax.broadcasted_iota(jnp.int32, (GRID, 256), 1)
+    for n, side in enumerate((1.0, -1.0)):
+        cut = slice(512 * n, 512 * n + 512)
+        x = trig + mask_r[:, cut]
+        average = jnp.mean(x, axis=1, keepdims=True)
+        spread = jnp.sum((x - average) * (x - average), axis=1, keepdims=True) * (1.0 / 1024)
+        products = gained(x, gain[:, cut], wh[cut, :])
+        full = jnp.concatenate([products, jnp.zeros((GRID, HD), F32)], axis=1)
+        full = jnp.where(at_lane == 192, 0.5 * average, full)
+        full = jnp.where(at_lane == 193, spread, full)
+        full = jnp.where(at_lane == 194, (0.5 * side) * average, full)
+        for i, term in enumerate(terms(full)):
+            ttab[96 * n + 32 * i : 96 * n + 32 * i + 32, :] = term
+
     def masked(i):
         r = rows(i, 256)
         owners = [(4 * i + j).astype(F32) for j in range(4)]
         row = jnp.concatenate([order_col(o) for o in owners], axis=0)
         col = jnp.concatenate([order_col(o + N) for o in owners], axis=0)
-        std, _ = norm(positions(row, col, True))
-        three = nn((std * gain).astype(BF16), wh[...]).astype(BF16)
+        sums = nn(row_and_col(row, col), ttab[...])
+        average, spread, apart = sums[:, 192:193], sums[:, 193:194], sums[:, 194:195]
+        inv = lax.rsqrt(spread + apart * apart + 1e-06)
+        three = ((sums[:, 0:192] - average * ones_gain) * inv).astype(BF16)
         qt[r, :] = three[:, 0:HD] * scale
         kt[r, :] = three[:, HD : 2 * HD]
         vt[r, :] = three[:, 2 * HD :]
@@ -248,11 +277,11 @@
             lt[b, r, :] = jnp.sum(e, axis=1, keepdims=True)
             acc[b, r, :] = nn(e.astype(BF16), vt[...])
 
-    loop(2, table)
+    loop(3, table)
     ids = jnp.concatenate(own_patch, axis=0).astype(jnp.int32)
-    xown[...] = positions((ids >> 5).astype(F32), (ids & 31).astype(F32), False)
-    own_position = positions(order_col(m.astype(F32)), order_col((m + N).astype(F32)), False)
-    pos[...] = own_position
+    xown[...] = positions((ids >> 5).astype(F32), (ids & 31).astype(F32))
+    pos[...] = positions(order_col(m.astype(F32)), order_col((m + N).astype(F32)))
+    encT[...] = jnp.transpose(enc[...])
 
     arrived(rsbuf.at[pl.ds(0, N - 1)], recv_s.at[0])
     rsbuf[m] = part[:, mine, :]
@@ -283,12 +312,10 @@
     each_peer(lambda k: to(k, qsend.at[k], qall.at[:, mine], send_s.at[1], recv_s.at[1]).start())
     qall[:, mine, :] = qsend[m]
 
-    lax.fori_loop(2, 4, lambda i, _: (table(i), 0)[1], 0)
-    encT[...] = jnp.transpose(enc[...])
+    table(3)
 
     arrived(qall.at[:, pl.ds(0, 240)], recv_s.at[1])
 
-    my_group = m // 4
 
     def attention(b):
         q, k, v = (qall[b, :, t * HD : (t + 1) * HD] for t in range(3))
@@ -448,9 +475,8 @@
         )
         for q in range(PIECES):
             ret[q, b, mine, :] = back[:, q * WIDE : (q + 1) * WIDE].astype(BF16)
-        for q in range(PIECES):
-            block = ret.at[q, b, mine]
-            each_peer(lambda k: to(k, block, block, ag2send.at[q, b], ag2_s.at[q, b]).start())
+        for block, sem in [(ret.at[:, 0, mine], (0, 0))] if b == 0 else [(ret.at[q, 1, mine], (q, 1)) for q in range(PIECES)]:
+            each_peer(lambda k: to(k, block, block, ag2send.at[sem], ag2_s.at[sem]).start())
 
     unrolled(2, norm_back)
 
@@ -468,9 +494,9 @@
 
     z_other = lax.rem(z + 1, NZ)
     firsts = [cross(loc.at[q, :, rows(1 - c, 192)], half_in.at[q], csend.at[q], crecv.at[q]) for q in range(PIECES)]
+    arrived(ret.at[:, 0, pl.ds(0, 240)], ag2_s.at[0, 0])
     for q in range(PIECES):
-        for b in range(2):
-            arrived(ret.at[q, b, pl.ds(0, 240)], ag2_s.at[q, b])
+        arrived(ret.at[q, 1, pl.ds(0, 240)], ag2_s.at[q, 1])
 
         def local_grad(t, q=q):
             both = nn(encT[...], ret[q, :, :, lanes(t, 256)].reshape(512, 256)).astype(BF16)
@@ -535,8 +561,9 @@
         left_here(attb.at[b, pl.ds(0, N - 1)], send_s.at[2 + b])
         left_here(gsend.at[b, pl.ds(0, N - 1)], send_s.at[4 + b])
         left_here(dbuf.at[b, pl.ds(0, N - 1)], send_s.at[6 + b])
-        for q in range(PIECES):
-            left_here(ret.at[q, b, pl.ds(0, 240)], ag2send.at[q, b])
+    left_here(ret.at[:, 0, pl.ds(0, 240)], ag2send.at[0, 0])
+    for q in range(PIECES):
+        left_here(ret.at[q, 1, pl.ds(0, 240)], ag2send.at[q, 1])
     for q in range(PIECES):
         firsts[q].wait_send()
         seven = zbuf.at[q, pl.ds(0, NZ - 1)]
@@ -570,7 +597,7 @@
         V((1024, 768), BF16), V((2, 64, 768), BF16),
         V((2, 256, 1024), BF16), V((N, 2, 16, 1024), BF16), V((384, 512), BF16),
         V((OWN, 2 * N), F32), V((2, 1, 1024), F32), V((2, 1024, 1), F32),
-        V((2, 1024, 256), BF16), V((2, 256, 1024), BF16), V((256, 1024), BF16),
+        V((2, 1024, 256), BF16), V((2, 256, 1024), BF16), V((192, 1024), BF16), V((192, 256), BF16),
         V((OWN, 1024), F32), V((32, 1024), F32), V((32, 1024), F32), V((32, 1), F32), V((1024, 192), BF16),
         V((1024, HD), BF16), V((1024, HD), BF16), V((1024, HD), BF16),
         V((2, 1024, 1), F32), V((2, 1024, 1), F32), V((2, 1024, HD), F32),

time: 104 us -> 105 us (level)
  no operation moved by 1% of the time
where the time goes in v5:
time: 105 us
  Pallas kernels  103 us (98%)
    pallas_call x1, Pallas kernels, body(): pl.pallas_call(kernel, out_shape=(jax.ShapeDtypeStruct((2, 64, 768), BF16...  101 us
    pallas_call x1, Pallas kernels, body(): pl.pallas_call(finish, out_shape=(jax.ShapeDtypeStruct((2, 64, 768), BF16...  2.72 us

profile of v5, /device:TPU:1, one launch (start us, length us, event | category | flops | bytes accessed | tf_op | source)
XLA Modules:
  0.0 104.8 jit_solution(9874020034344158097)
XLA Ops:
  0.6 0.1 fusion.1
  0.8 0.6 pad_maximum_fusion.trig_r
  1.4 100.7 %shard_map.139 = (bf16[2,64,768]{2,1,0:T(8,128)(2,1)}, bf16[512,384]{1,0:T(8,128)(2,1)}, bf16[384,1024]{1,0:T(8,128)(2,1)}) custom-call(bf16[512,384]{1,0:T(8,128)(2,1)} %enc_h.1, bf16[384,1024]{1,0:T(8,128)(2,1)} %we_h.1, s32[1,1024]{1,0:T(1,128)} %bitcast.3, s32[2,256]{1,0:T(2,128)} %vis_r.1, f32[1,1024]{1,0:T(1,128)} %bitcast.4, f32[1,1024]{1,0:T(1,128)} %bitcast.5, ...), custom_call_target="tpu_custom_call" | custom-call | flops 8000000000 | bytes 16000000 | tf_op jit(solution)/shard_map/pallas_call | solution.py:617
  102.1 2.7 %shard_map.140 = (bf16[2,64,768]{2,1,0:T(8,128)(2,1)}, bf16[512,384]{1,0:T(8,128)(2,1)}, f32[384,1024]{1,0:T(8,128)}) custom-call(bf16[2,64,768]{2,1,0:T(8,128)(2,1)} %get-tuple-element.6.pred_i, bf16[512,384]{1,0:T(8,128)(2,1)} %get-tuple-element.7.encg_i, bf16[384,1024]{1,0:T(8,128)(2,1)} %get-tuple-element.8.emb_i), custom_call_target="tpu_custom_call" | custom-call | flops 400000 | bytes 3500000 | tf_op jit(solution)/shard_map/pallas_call | solution.py:635
  (1 shorter events, 0.0 us)

commit v6 on v5

--- a/solution.py
+++ b/solution.py
@@ -73,13 +73,13 @@
     enc_h, we_h, own_r, vis_r, mask_r, gain_r, wq_h, wk_h, wv_h, wo_h, wp_h, tgt_h, trig_r,
     pred_o, encg_o, emb_o,
     enc, we, wq, wk, wv, wo, wp, tgt,
-    part, rsbuf, encT,
+    part, rsbuf, rsbuf2, line, encT,
     order, seenrow, seencol, put, take, ptab, ttab, pos, xown, stdo, invo, wh,
     qt, kt, vt, mt, lt, acc,
     normed, fs, qsend, qall, av, ave, p1s, p2s, ps,
     attp, attb, attf, ef, updb, resid, gub, gab, gsend, gall, dpack, dbuf, df, sc, ret,
     loc, half_in, zin, zbuf, zgat, zown,
-    lsem, send_s, recv_s, ag2send, ag2_s, zsend, z1_s, z2send, z2_s, csend, crecv, fsend, frecv,
+    lsem, one_s, one_r, two_s, two_r, send_s, recv_s, ag2send, ag2_s, zsend, z1_s, z2send, z2_s, csend, crecv, fsend, frecv,
 ):
     m = lax.axis_index("mp")
     z = lax.axis_index("dp")
@@ -128,33 +128,43 @@
 
     loads[0].wait()
     loads[1].wait()
+
+    mx, my = m // 4, lax.rem(m, 4)
+    first_at, second_at = (mx, my), (my, mx)
+
+    def device(half, along_first, along_second):
+        return 4 * along_first + along_second if half == 0 else 4 * along_second + along_first
 
     def partial_block(g):
         both = jnp.concatenate(
             [enc[rows(g, 64), :], enc[pl.ds(pl.multiple_of(256 + g * 64, 64), 64), :]], axis=0
         )
         out = nn(both, we[...]).astype(BF16)
-        part[0, rows(g, 64), :] = out[:64]
-        part[1, rows(g, 64), :] = out[64:]
-
-    my_group = m // 4
-
-    def send_part(k):
-        to(k, part.at[:, rows(k, 16)], rsbuf.at[m], send_s.at[0], recv_s.at[0]).start()
-
-    partial_block(lax.rem(my_group + 1, 4))
+        for b in range(2):
+            part[0, b, rows(g, 64), :] = out[b * 64 : (b + 1) * 64, 0:512]
+            for y in range(4):
+                at = pl.ds(pl.multiple_of(y * 64 + g * 16, 16), 16)
+                part[1, b, at, :] = out[b * 64 + y * 16 : b * 64 + (y + 1) * 16, 512:1024]
+
+    def send_first(half, to_line):
+        to(
+            device(half, to_line, second_at[half]), part.at[half, :, rows(to_line, 64)],
+            rsbuf.at[half, first_at[half]], one_s.at[half], one_r.at[half],
+        ).start()
+
+    partial_block(lax.rem(mx + 1, 4))
     pl.semaphore_wait(barrier, N - 1 + NZ - 1 + 1)
 
     def send_group(jj, _):
-        g = lax.rem(my_group + jj, 4)
-        for i in range(4):
-            send_part(4 * g + i)
+        g = lax.rem(mx + jj, 4)
+        send_first(0, g)
         partial_block(lax.rem(g + 1, 4))
         return 0
 
     lax.fori_loop(1, 4, send_group, 0)
-    for i in range(1, 4):
-        send_part(4 * my_group + lax.rem(m + i, 4))
+    for j in range(1, 4):
+        send_first(1, lax.rem(my + j, 4))
+    my_group = mx
 
     owner_row = own_r[...].astype(F32)
     of_owner = jnp.where(owner_row == fiota((N, 1024), 0), 1.0, 0.0)
@@ -277,17 +287,39 @@
             lt[b, r, :] = jnp.sum(e, axis=1, keepdims=True)
             acc[b, r, :] = nn(e.astype(BF16), vt[...])
 
-    loop(3, table)
+    table(0)
+
+    for half in range(2):
+        here = first_at[half]
+        arrived(rsbuf.at[half, pl.ds(0, 3)], one_r.at[half])
+        rsbuf[half, here] = part[half, :, rows(here, 64), :]
+        total = rsbuf[half, 0].astype(F32)
+        for a in range(1, 4):
+            total = total + rsbuf[half, a].astype(F32)
+        line[half] = total.astype(BF16)
+        for j in range(1, 4):
+            there = lax.rem(second_at[half] + j, 4)
+            to(
+                device(half, here, there), line.at[half, :, rows(there, 16)],
+                rsbuf2.at[half, second_at[half]], two_s.at[half], two_r.at[half],
+            ).start()
+
+    lax.fori_loop(1, 3, lambda i, _: (table(i), 0)[1], 0)
     ids = jnp.concatenate(own_patch, axis=0).astype(jnp.int32)
     xown[...] = positions((ids >> 5).astype(F32), (ids & 31).astype(F32))
     pos[...] = positions(order_col(m.astype(F32)), order_col((m + N).astype(F32)))
     encT[...] = jnp.transpose(enc[...])
 
-    arrived(rsbuf.at[pl.ds(0, N - 1)], recv_s.at[0])
-    rsbuf[m] = part[:, mine, :]
-    own_rows = lax.fori_loop(
-        0, N, lambda k, total: total + rsbuf[k].astype(F32), jnp.zeros((2, 16, 1024), F32)
-    ).reshape(32, 1024)
+    own_rows = []
+    for half in range(2):
+        here = second_at[half]
+        arrived(rsbuf2.at[half, pl.ds(0, 3)], two_r.at[half])
+        rsbuf2[half, here] = line[half, :, rows(here, 16), :]
+        total = rsbuf2[half, 0].astype(F32)
+        for a in range(1, 4):
+            total = total + rsbuf2[half, a].astype(F32)
+        own_rows.append(total.reshape(32, 512))
+    own_rows = jnp.concatenate(own_rows, axis=1)
     std, inv = norm(own_rows + xown[...])
     stdo[...] = std
     invo[...] = inv
@@ -555,7 +587,9 @@
             forward(q, k).wait_recv()
         write(q, 1 - c, zown)
 
-    left_here(rsbuf.at[pl.ds(0, N - 1)], send_s.at[0])
+    for half in range(2):
+        left_here(rsbuf.at[half, pl.ds(0, 3)], one_s.at[half])
+        left_here(rsbuf2.at[half, pl.ds(0, 3)], two_s.at[half])
     left_here(qsend.at[pl.ds(0, N - 1)], send_s.at[1])
     for b in range(2):
         left_here(attb.at[b, pl.ds(0, N - 1)], send_s.at[2 + b])
@@ -595,7 +629,7 @@
         V((512, 384), BF16), V((384, 1024), BF16),
         V((1024, 1024), BF16), V((1024, 1024), BF16), V((1024, 1024), BF16), V((1024, 1024), BF16),
         V((1024, 768), BF16), V((2, 64, 768), BF16),
-        V((2, 256, 1024), BF16), V((N, 2, 16, 1024), BF16), V((384, 512), BF16),
+        V((2, 2, 256, 512), BF16), V((2, 4, 2, 64, 512), BF16), V((2, 4, 2, 16, 512), BF16), V((2, 2, 64, 512), BF16), V((384, 512), BF16),
         V((OWN, 2 * N), F32), V((2, 1, 1024), F32), V((2, 1024, 1), F32),
         V((2, 1024, 256), BF16), V((2, 256, 1024), BF16), V((192, 1024), BF16), V((192, 256), BF16),
         V((OWN, 1024), F32), V((32, 1024), F32), V((32, 1024), F32), V((32, 1), F32), V((1024, 192), BF16),
@@ -610,7 +644,7 @@
         V((PIECES, TILES, 384, 128), BF16), V((PIECES, TILES, 192, 128), BF16),
         V((PIECES, NZ, DEEP, 128), BF16), V((PIECES, NZ, DEEP, 128), BF16),
         V((PIECES, NZ, DEEP, 128), BF16), V((PIECES, NZ, DEEP, 128), BF16),
-        dma((8,)), dma((8,)), dma((8,)), dma((PIECES, 2)), dma((PIECES, 2)),
+        dma((8,)), dma((2,)), dma((2,)), dma((2,)), dma((2,)), dma((8,)), dma((8,)), dma((PIECES, 2)), dma((PIECES, 2)),
         dma((PIECES,)), dma((PIECES,)), dma((PIECES,)), dma((PIECES, NZ)),
         dma((PIECES,)), dma((PIECES,)), dma((PIECES, NZ)), dma((PIECES, NZ)),
     ]

time: 105 us -> 99.7 us (0.950)
  Pallas kernels: 103 us -> 98.1 us
    pallas_call x1, Pallas kernels: 101 us -> 95.4 us  [body(): pl.pallas_call(kernel, out_shape=(jax.ShapeDtypeStruct((2, 64, 768), BF16...]
where the time goes in v6:
time: 99.7 us; the launch traced here: 99.5 us
  Pallas kernels  98.1 us (98%)
    pallas_call x1, Pallas kernels, body(): pl.pallas_call(kernel, out_shape=(jax.ShapeDtypeStruct((2, 64, 768), BF16...  95.4 us
    pallas_call x1, Pallas kernels, body(): pl.pallas_call(finish, out_shape=(jax.ShapeDtypeStruct((2, 64, 768), BF16...  2.72 us

profile of v6, /device:TPU:1, one launch (start us, length us, event | category | flops | bytes accessed | tf_op | source)
XLA Modules:
  0.0 99.5 jit_solution(13007805878226815530)
XLA Ops:
  0.6 0.1 fusion.1
  0.8 0.6 pad_maximum_fusion.trig_r
  1.4 95.4 %shard_map.139 = (bf16[2,64,768]{2,1,0:T(8,128)(2,1)}, bf16[512,384]{1,0:T(8,128)(2,1)}, bf16[384,1024]{1,0:T(8,128)(2,1)}) custom-call(bf16[512,384]{1,0:T(8,128)(2,1)} %enc_h.1, bf16[384,1024]{1,0:T(8,128)(2,1)} %we_h.1, s32[1,1024]{1,0:T(1,128)} %bitcast.3, s32[2,256]{1,0:T(2,128)} %vis_r.1, f32[1,1024]{1,0:T(1,128)} %bitcast.4, f32[1,1024]{1,0:T(1,128)} %bitcast.5, ...), custom_call_target="tpu_custom_call" | custom-call | flops 8000000000 | bytes 16000000 | tf_op jit(solution)/shard_map/pallas_call | solution.py:651
  96.8 2.7 %shard_map.140 = (bf16[2,64,768]{2,1,0:T(8,128)(2,1)}, bf16[512,384]{1,0:T(8,128)(2,1)}, f32[384,1024]{1,0:T(8,128)}) custom-call(bf16[2,64,768]{2,1,0:T(8,128)(2,1)} %get-tuple-element.6.pred_i, bf16[512,384]{1,0:T(8,128)(2,1)} %get-tuple-element.7.encg_i, bf16[384,1024]{1,0:T(8,128)(2,1)} %get-tuple-element.8.emb_i), custom_call_target="tpu_custom_call" | custom-call | flops 400000 | bytes 3500000 | tf_op jit(solution)/shard_map/pallas_call | solution.py:669
  (1 shorter events, 0.0 us)

commit v7 on v6

--- a/solution.py
+++ b/solution.py
@@ -70,7 +70,7 @@
 
 
 def kernel(
-    enc_h, we_h, own_r, vis_r, mask_r, gain_r, wq_h, wk_h, wv_h, wo_h, wp_h, tgt_h, trig_r,
+    enc_h, we_h, own_r, vis_r, mask_r, gain_r, wq_h, wk_h, wv_h, wo_h, wp_h, tgt_h, sin_r, cos_r,
     pred_o, encg_o, emb_o,
     enc, we, wq, wk, wv, wo, wp, tgt,
     part, rsbuf, rsbuf2, line, encT,
@@ -79,7 +79,7 @@
     normed, fs, qsend, qall, av, ave, p1s, p2s, ps,
     attp, attb, attf, ef, updb, resid, gub, gab, gsend, gall, dpack, dbuf, df, sc, ret,
     loc, half_in, zin, zbuf, zgat, zown,
-    lsem, one_s, one_r, two_s, two_r, send_s, recv_s, ag2send, ag2_s, zsend, z1_s, z2send, z2_s, csend, crecv, fsend, frecv,
+    lsem, one_s, one_r, two_s, two_r, send_s, recv_s, ag1send, ag1_s, ag2send, ag2_s, zsend, z1_s, z2send, z2_s, csend, crecv, fsend, frecv,
 ):
     m = lax.axis_index("mp")
     z = lax.axis_index("dp")
@@ -218,7 +218,7 @@
         mid = rest.astype(BF16)
         return hi, mid, (rest - mid.astype(F32)).astype(BF16)
 
-    trig = trig_r[...]
+    trig = jnp.concatenate([sin_r[...], cos_r[...]], axis=1)
     ptab[...] = jnp.zeros_like(ptab)
     for i, term in enumerate(terms(trig)):
         ptab[32 * i : 32 * i + 32, 0:512] = term
@@ -483,6 +483,8 @@
 
     def norm_back(b):
         arrived(dbuf.at[b, pl.ds(0, N - 1)], recv_s.at[6 + b])
+        if b == 1:
+            pass_lines(0)
 
         def unpack(i):
             one, two = dbuf[b, 2 * i], dbuf[b, 2 * i + 1]
@@ -506,11 +508,23 @@
             - std * jnp.mean(scaled * std, axis=-1, keepdims=True)
         )
         for q in range(PIECES):
-            ret[q, b, mine, :] = back[:, q * WIDE : (q + 1) * WIDE].astype(BF16)
-        for block, sem in [(ret.at[:, 0, mine], (0, 0))] if b == 0 else [(ret.at[q, 1, mine], (q, 1)) for q in range(PIECES)]:
-            each_peer(lambda k: to(k, block, block, ag2send.at[sem], ag2_s.at[sem]).start())
+            ret[q, b, mx, my] = back[:, q * WIDE : (q + 1) * WIDE].astype(BF16)
+        for q in range(PIECES):
+            block = ret.at[q, b, mx, my]
+            for j in range(1, 4):
+                there = lax.rem(first_at[q] + j, 4)
+                to(device(q, there, second_at[q]), block, block, ag1send.at[q, b], ag1_s.at[q, b]).start()
+
+    def pass_lines(b):
+        for q in range(PIECES):
+            arrived(ret.at[q, b, 0, pl.ds(0, 3)], ag1_s.at[q, b])
+            line_of = ret.at[q, b, :, my] if q == 0 else ret.at[q, b, mx]
+            for j in range(1, 4):
+                there = lax.rem(second_at[q] + j, 4)
+                to(device(q, first_at[q], there), line_of, line_of, ag2send.at[q, b], ag2_s.at[q, b]).start()
 
     unrolled(2, norm_back)
+    pass_lines(1)
 
     def cross(src, dst, send, recv):
         return pltpu.make_async_remote_copy(
@@ -526,12 +540,12 @@
 
     z_other = lax.rem(z + 1, NZ)
     firsts = [cross(loc.at[q, :, rows(1 - c, 192)], half_in.at[q], csend.at[q], crecv.at[q]) for q in range(PIECES)]
-    arrived(ret.at[:, 0, pl.ds(0, 240)], ag2_s.at[0, 0])
     for q in range(PIECES):
-        arrived(ret.at[q, 1, pl.ds(0, 240)], ag2_s.at[q, 1])
+        for b in range(2):
+            arrived(ret.at[q, b, pl.ds(0, 3)], ag2_s.at[q, b])
 
         def local_grad(t, q=q):
-            both = nn(encT[...], ret[q, :, :, lanes(t, 256)].reshape(512, 256)).astype(BF16)
+            both = nn(encT[...], ret[q, :, :, :, :, lanes(t, 256)].reshape(512, 256)).astype(BF16)
             loc[q, 2 * t] = both[:, :128]
             loc[q, 2 * t + 1] = both[:, 128:]
 
@@ -562,9 +576,9 @@
         forward(q, z).start()
 
     def encoder_grad(b):
-        total = nt(ret[0, b], we[:, 0:WIDE])
+        total = nt(ret[0, b].reshape(256, WIDE), we[:, 0:WIDE])
         for q in range(1, PIECES):
-            total = total + nt(ret[q, b], we[:, q * WIDE : (q + 1) * WIDE])
+            total = total + nt(ret[q, b].reshape(256, WIDE), we[:, q * WIDE : (q + 1) * WIDE])
         encg_o[rows(b, 256), :] = total.astype(BF16)
 
     unrolled(2, encoder_grad)
@@ -595,9 +609,10 @@
         left_here(attb.at[b, pl.ds(0, N - 1)], send_s.at[2 + b])
         left_here(gsend.at[b, pl.ds(0, N - 1)], send_s.at[4 + b])
         left_here(dbuf.at[b, pl.ds(0, N - 1)], send_s.at[6 + b])
-    left_here(ret.at[:, 0, pl.ds(0, 240)], ag2send.at[0, 0])
     for q in range(PIECES):
-        left_here(ret.at[q, 1, pl.ds(0, 240)], ag2send.at[q, 1])
+        for b in range(2):
+            left_here(ret.at[q, b, 0, pl.ds(0, 3)], ag1send.at[q, b])
+            left_here(ret.at[q, b, pl.ds(0, 3)], ag2send.at[q, b])
     for q in range(PIECES):
         firsts[q].wait_send()
         seven = zbuf.at[q, pl.ds(0, NZ - 1)]
@@ -620,7 +635,6 @@
     quarter = 256
     freqs = 10000.0 ** (-jnp.arange(quarter, dtype=F32) / quarter)
     angle = jnp.arange(GRID, dtype=F32)[:, None] * freqs[None, :]
-    trig = jnp.concatenate([jnp.sin(angle), jnp.cos(angle)], axis=1)
     vm = pl.BlockSpec(memory_space=pltpu.VMEM)
     hbm = pl.BlockSpec(memory_space=pl.ANY)
     V = pltpu.VMEM
@@ -640,11 +654,11 @@
         V((2, 1024, 128), BF16), V((2, N, 64, 128), BF16), V((64, 1024), BF16), V((64, 1024), BF16),
         V((64, 1024), BF16), V((64, 768), BF16), V((64, 1024), BF16), V((64, 1024), BF16),
         V((2, N, 64, 128), BF16), V((2, 1024, 128), BF16), V((2, 256, 256), BF16), V((2, N, 16, 256), BF16),
-        V((4, 16, 1024), BF16), V((16, 1024), F32), V((PIECES, 2, 256, WIDE), BF16),
+        V((4, 16, 1024), BF16), V((16, 1024), F32), V((PIECES, 2, 4, 4, 16, WIDE), BF16),
         V((PIECES, TILES, 384, 128), BF16), V((PIECES, TILES, 192, 128), BF16),
         V((PIECES, NZ, DEEP, 128), BF16), V((PIECES, NZ, DEEP, 128), BF16),
         V((PIECES, NZ, DEEP, 128), BF16), V((PIECES, NZ, DEEP, 128), BF16),
-        dma((8,)), dma((2,)), dma((2,)), dma((2,)), dma((2,)), dma((8,)), dma((8,)), dma((PIECES, 2)), dma((PIECES, 2)),
+        dma((8,)), dma((2,)), dma((2,)), dma((2,)), dma((2,)), dma((8,)), dma((8,)), dma((PIECES, 2)), dma((PIECES, 2)), dma((PIECES, 2)), dma((PIECES, 2)),
         dma((PIECES,)), dma((PIECES,)), dma((PIECES,)), dma((PIECES, NZ)),
         dma((PIECES,)), dma((PIECES,)), dma((PIECES, NZ)), dma((PIECES, NZ)),
     ]
@@ -655,7 +669,7 @@
             jax.ShapeDtypeStruct((512, 384), BF16),
             jax.ShapeDtypeStruct((384, 1024), BF16),
         ),
-        in_specs=[hbm, hbm, vm, vm, vm, vm, hbm, hbm, hbm, hbm, hbm, hbm, vm],
+        in_specs=[hbm, hbm, vm, vm, vm, vm, hbm, hbm, hbm, hbm, hbm, hbm, vm, vm],
         out_specs=(vm, vm, vm),
         scratch_shapes=scratch,
         compiler_params=pltpu.CompilerParams(
@@ -664,7 +678,7 @@
         cost_estimate=pl.CostEstimate(flops=8_000_000_000, bytes_accessed=16_000_000, transcendentals=4_000_000),
     )(
         encoded, embed_weight, owner.reshape(1, 1024), visible, mask_token.reshape(1, 1024), norm_gain.reshape(1, 1024),
-        query_weight, key_weight, value_weight, out_weight, pixel_weight, targets, trig,
+        query_weight, key_weight, value_weight, out_weight, pixel_weight, targets, jnp.sin(angle), jnp.cos(angle),
     )
     return pl.pallas_call(
         finish,

time: 99.7 us -> 103 us (1.033)
  Pallas kernels: 98.1 us -> 102 us
    pallas_call x1, Pallas kernels: 95.4 us -> 98.8 us  [body(): pl.pallas_call(kernel, out_shape=(jax.ShapeDtypeStruct((2, 64, 768), BF16...]
where the time goes in v7:
time: 103 us
  Pallas kernels  102 us (99%)
    pallas_call x1, Pallas kernels, body(): pl.pallas_call(kernel, out_shape=(jax.ShapeDtypeStruct((2, 64, 768), BF16...  98.8 us
    pallas_call x1, Pallas kernels, body(): pl.pallas_call(finish, out_shape=(jax.ShapeDtypeStruct((2, 64, 768), BF16...  2.72 us

profile of v7, /device:TPU:1, one launch (start us, length us, event | category | flops | bytes accessed | tf_op | source)
XLA Modules:
  0.0 103.0 jit_solution(10711929830112491254)
XLA Ops:
  0.6 0.8 fusion
  1.4 98.8 %shard_map.139 = (bf16[2,64,768]{2,1,0:T(8,128)(2,1)}, bf16[512,384]{1,0:T(8,128)(2,1)}, bf16[384,1024]{1,0:T(8,128)(2,1)}) custom-call(bf16[512,384]{1,0:T(8,128)(2,1)} %enc_h.1, bf16[384,1024]{1,0:T(8,128)(2,1)} %we_h.1, s32[1,1024]{1,0:T(1,128)} %bitcast.3, s32[2,256]{1,0:T(2,128)} %vis_r.1, f32[1,1024]{1,0:T(1,128)} %bitcast.4, f32[1,1024]{1,0:T(1,128)} %bitcast.5, ...), custom_call_target="tpu_custom_call" | custom-call | flops 8000000000 | bytes 16000000 | tf_op jit(solution)/shard_map/pallas_call | solution.py:665
  100.2 2.7 %shard_map.140 = (bf16[2,64,768]{2,1,0:T(8,128)(2,1)}, bf16[512,384]{1,0:T(8,128)(2,1)}, f32[384,1024]{1,0:T(8,128)}) custom-call(bf16[2,64,768]{2,1,0:T(8,128)(2,1)} %get-tuple-element.6.pred_i, bf16[512,384]{1,0:T(8,128)(2,1)} %get-tuple-element.7.encg_i, bf16[384,1024]{1,0:T(8,128)(2,1)} %get-tuple-element.8.emb_i), custom_call_target="tpu_custom_call" | custom-call | flops 400000 | bytes 3500000 | tf_op jit(solution)/shard_map/pallas_call | solution.py:683
  (1 shorter events, 0.0 us)
